TPU v7x, 32 devices: a whole 2x2x4 slice. The times are simulated.
32 devices in a mesh: section: 4 (over y, x), half: 2 (over core), dp: 4 (over z).
Axes of the slice: x: 2, y: 2, z: 4, core: 2. Of those that a mesh axis runs over, the one named last changes fastest.
Arguments:
- query: bfloat16 [64, 12288], P('dp', ('section', 'half')), may hold values from -6 to 6
- train: bfloat16 [4096, 12288], P('dp', ('section', 'half')), may hold values from -0.0546875 to 0.0546875
- precond: bfloat16 [48, 256, 256], P(('section', 'half')), may hold values from -0.375 to 0.375
- module_kind: int32 [48], P(('section', 'half')), may hold values from 0 to 6
- kind_scale: float32 [7], replicated, may hold values from 0.25 to 4
Outputs:
- scores: float32 [64, 4096], P(('section', 'half'), 'dp')
All inputs are finite; a program needn't handle non-finite values.
Results may differ from a plain program's by a relative error of at most 0.0029.
Values may be sent and summed in bfloat16 or wider, within the bound.
No kernel may reach another device: no remote copies, remote signals or barrier semaphores. Data moves between devices by JAX's collectives and lax.ppermute only.
A program may use at most 64 MiB of HBM per device.

v0:
```python
import jax
import jax.numpy as jnp
from jax import lax
from jax.sharding import PartitionSpec as P


def per_device(query, train, precond, module_kind, kind_scale):
    q_rows = query.shape[0]
    mods = precond.shape[0]
    feat = precond.shape[1]
    blocks = query.reshape(q_rows, mods, feat)
    pre = jnp.einsum("qmf,mfg->qmg", blocks, precond, preferred_element_type=jnp.float32)
    kinds = jnp.arange(kind_scale.shape[0], dtype=jnp.int32)
    onehot = (module_kind[:, None] == kinds[None, :]).astype(jnp.float32)
    factor = jnp.sum(onehot * kind_scale[None, :], axis=1)
    weighted = (pre * factor[None, :, None]).astype(jnp.bfloat16).reshape(q_rows, mods * feat)
    gathered = lax.dot_general(
        lax.all_gather(weighted, "dp", axis=0, tiled=True),
        train,
        (((1,), (1,)), ((), ())),
        preferred_element_type=jnp.float32,
    )
    return lax.psum_scatter(gathered, ("section", "half"), scatter_dimension=0, tiled=True)


def solution(mesh):
    in_specs = (
        P("dp", ("section", "half")),
        P("dp", ("section", "half")),
        P(("section", "half"), None, None),
        P(("section", "half")),
        P(),
    )
    out_specs = P(("section", "half"), "dp")
    return jax.shard_map(
        per_device, mesh=mesh, in_specs=in_specs, out_specs=out_specs, check_vma=False
    )
```

profile of v0, /device:TPU:0, one launch (start us, length us, event | category | flops | bytes accessed | tf_op | source)
XLA Modules:
  0.0 68.0 jit_solution(14577265279454461789)
XLA Ops:
  6.5 0.0 copy-start
  6.5 0.0 reduce-scatter.2.cloned.1.call-start
  6.5 1.0 %select_reduce_fusion = f32[6]{0:T(128)S(1)} fusion(f32[7]{0:T(128)} %param.9, s32[6]{0:T(128)} %param.8), kind=kLoop, calls=%fused_computation.5 | loop fusion | flops 120 | bytes 76 | tf_op jit(solution)/shard_map/reduce_sum | solution.py:15
  7.5 1.4 %fusion.1 = bf16[6,2,8,256]{3,2,1,0:T(8,128)(2,1)S(1)} fusion(bf16[6,256,256]{2,1,0:T(8,128)(2,1)} %param.7, bf16[2,6,8,256]{3,2,1,0:T(8,128)(2,1)} %bitcast.12, f32[6]{0:T(128)S(1)} %select_reduce_fusion), kind=kOutput, calls=%fused_computation.2 | convolution fusion | flops 12632064 | bytes 884760 | tf_op jit(solution)/shard_map/qmf,mfg->qmg/dot_general | solution.py:12
  8.9 15.5 %all_gather.3 = bf16[64,1536]{1,0:T(8,128)(2,1)S(1)} all-gather(bf16[16,1536]{1,0:T(8,128)(2,1)S(1)} %bitcast.11), channel_id=1, replica_groups=mesh['section'=4,'half'=2,'dp'=4] {'dp'}, dimensions={0}, use_global_device_ids=true | all-gather | bytes 245760 | tf_op jit(solution)/shard_map/all_gather | solution.py:18
  24.4 0.0 copy-done
  24.4 1.8 %fusion.4 = f32[64,1024]{1,0:T(8,128)} fusion(bf16[64,1536]{1,0:T(8,128)(2,1)S(1)} %all_gather.3, bf16[1024,1536]{1,0:T(8,128)(2,1)S(1)} %copy-done), kind=kOutput, calls=%fused_computation.7 | convolution fusion | flops 201326592 | bytes 3604480 | tf_op jit(solution)/shard_map/dot_general | solution.py:17
  26.1 0.0 reduce-scatter.2.cloned.1.call-update
  26.2 35.0 %reduce-scatter.2.cloned.1.call-done = f32[8,1024]{1,0:T(8,128)} async-done(((f32[64,1024]{1,0:T(8,128)}), f32[8,1024]{1,0:T(8,128)}) %reduce-scatter.2.cloned.1.call-update) | async-done | bytes 32784 | tf_op jit(solution)/shard_map/reduce_scatter | solution.py:23
  (1 shorter events, 0.0 us)
Async XLA Ops:
  6.5 17.9 %copy-start = (bf16[1024,1536]{1,0:T(8,128)(2,1)S(1)}, bf16[1024,1536]{1,0:T(8,128)(2,1)}, u32[]{:S(2)}) copy-start(bf16[1024,1536]{1,0:T(8,128)(2,1)} %param.6) | copy-start | bytes 9437188
  6.5 54.7 %reduce-scatter.2.cloned.1.call-start = ((), (), s32[]{:S(2)}) async-start(), calls=%async_computation.1 | async-start | bytes 294912 | tf_op jit(solution)/shard_map/reduce_scatter | solution.py:23
Sparse Core Ops, SparseCore 0:
  26.3 34.8 reduce-scatter.1
where the time goes:
time: 68.2 us; the launch traced here: 68 us
  waiting for transfers between devices  35 us (51%)
  blocking collectives  15.5 us (23%)
  between operations  13.4 us (20%)
  matrix products  3.12 us (5%)
  other arithmetic  1 us (1%)
    reduce_scatter x1, waiting for transfers between devices, per_device(): lax.psum_scatter(gathered, ('section', 'half'), scatter_dimension=0, tile...  35 us
    all_gather x1, blocking collectives, per_device(): lax.all_gather(weighted, 'dp', axis=0, tiled=True)  15.5 us
    dot_general x1, matrix products, per_device(): lax.dot_general(lax.all_gather(weighted, 'dp', axis=0, tiled=True), train...  1.75 us
    dot_general x1, matrix products, per_device(): jnp.einsum('qmf,mfg->qmg', blocks, precond, preferred_element_type=jnp.fl...  1.36 us
  transfers between devices with their start and end apart: 1, of which 1 were waited for; matrix products, arithmetic and copies ran while one was open for 0% of the time, Pallas kernels for 0%

commit v1 on v0

v1 whole, which is shorter than its diff:
```python
import functools

import jax
import jax.numpy as jnp
from jax import lax
from jax.experimental import pallas as pl
from jax.experimental.pallas import tpu as pltpu
from jax.sharding import PartitionSpec as P

SHARDS = ("section", "half")
DIRECT = 8
ROWS = 64


def local_scores(n, sections, halves, direct, *refs):
    blocks = refs[:n] if direct else refs[:1]
    train, precond, factor, keep, send = refs[len(blocks):]
    mods, feat = precond.shape[0], precond.shape[1]
    q_rows = blocks[0].shape[0] if direct else blocks[0].shape[0] // n
    out_rows = keep.shape[1]
    unit = min(q_rows, out_rows)
    dp, section, half = lax.axis_index("dp"), lax.axis_index("section"), lax.axis_index("half")

    def rows_of(first, rows, owners):
        parts = []
        for m in range(mods):
            cols = slice(m * feat, (m + 1) * feat)
            lhs = first(cols)
            pre = jnp.dot(lhs, precond[m], preferred_element_type=jnp.float32)
            parts.append((pre * factor[m]).astype(jnp.bfloat16))
        weighted = jnp.concatenate(parts, axis=1)
        scores = lax.dot_general(weighted, train[...], (((1,), (1,)), ((), ())), preferred_element_type=jnp.float32)
        for i in range(rows // unit):
            g = owners(i * unit)
            d, off = g // out_rows, pl.multiple_of(g % out_rows, unit)
            slot = lax.rem(d // halves, sections) ^ section
            value = scores[i * unit:(i + 1) * unit]
            mine = lax.rem(d, halves) == half

            @pl.when(mine)
            def _():
                keep[slot, pl.ds(off, unit), :] = value

            @pl.when(jnp.logical_not(mine))
            def _():
                send[slot, pl.ds(off, unit), :] = value

    if direct:
        first = lambda cols: jnp.concatenate([b[:, cols] for b in blocks], axis=0)
        rows_of(first, n * q_rows, lambda r: lax.rem(dp - r // q_rows + n, n) * q_rows + r % q_rows)
    else:
        def step(c, carry):
            base = pl.multiple_of(c * ROWS, ROWS)
            rows_of(lambda cols: blocks[0][pl.ds(base, ROWS), cols], ROWS, lambda r: base + r)
            return carry
        lax.fori_loop(0, n * q_rows // ROWS, step, 0)


def stage(train, precond, kind, scale, train_out, precond_out, factor_out, kind_s, scale_s, sems):
    pairs = ((kind, kind_s), (scale, scale_s), (precond, precond_out), (train, train_out))
    copies = [pltpu.make_async_copy(src, dst, sems.at[i]) for i, (src, dst) in enumerate(pairs)]
    for c in copies:
        c.start()
    copies[0].wait()
    copies[1].wait()
    for m in range(factor_out.shape[0]):
        factor_out[m] = jnp.full(factor_out.shape[1:], scale_s[kind_s[m]], jnp.float32)
    copies[2].wait()
    copies[3].wait()


def per_device(query, train, precond, module_kind, kind_scale):
    n, sections, halves = (lax.axis_size(a) for a in ("dp", "section", "half"))
    q_rows = query.shape[0]
    out_rows = n * q_rows // (sections * halves)
    direct = n <= DIRECT
    if direct:
        blocks = [query] + [lax.ppermute(query, "dp", [(i, (i + s) % n) for i in range(n)]) for s in range(1, n)]
    else:
        blocks = [lax.all_gather(query, "dp", axis=0, tiled=True)]
    mods, feat = precond.shape[:2]
    vmem, hbm = (pl.BlockSpec(memory_space=s) for s in (pltpu.VMEM, pltpu.HBM))
    staged = pl.pallas_call(
        stage,
        out_shape=(
            pltpu.VMEM(train.shape, train.dtype),
            pltpu.VMEM(precond.shape, precond.dtype),
            pltpu.VMEM((mods, 1, feat), jnp.float32),
        ),
        in_specs=[hbm] * 4,
        out_specs=(vmem,) * 3,
        scratch_shapes=[
            pltpu.SMEM(module_kind.shape, module_kind.dtype),
            pltpu.SMEM(kind_scale.shape, kind_scale.dtype),
            pltpu.SemaphoreType.DMA((4,)),
        ],
        cost_estimate=pl.CostEstimate(flops=0, bytes_accessed=2 * train.size * 2, transcendentals=0),
        compiler_params=pltpu.CompilerParams(vmem_limit_bytes=32 * 2**20),
        name="stage",
    )(*(pltpu.with_memory_space_constraint(a, pltpu.HBM) for a in (train, precond, module_kind, kind_scale)))
    part = jax.ShapeDtypeStruct((sections, out_rows, train.shape[0]), jnp.float32)
    keep, send = pl.pallas_call(
        functools.partial(local_scores, n, sections, halves, direct),
        out_shape=(part, part),
        in_specs=[vmem] * (len(blocks) + 3),
        out_specs=(vmem, vmem),
        compiler_params=pltpu.CompilerParams(vmem_limit_bytes=48 * 2**20),
        name="local_scores",
    )(*blocks, *staged)
    got = lax.ppermute(send, "half", [(i, 1 - i) for i in range(halves)])
    both = keep + got
    out = both[0]
    for s in range(1, sections):
        moved = lax.ppermute(both[s].astype(RT), "section", [(i, i ^ s) for i in range(sections)])
        out = out + moved.astype(jnp.float32)
    return out


RT = jnp.bfloat16


def solution(mesh):
    in_specs = (
        P("dp", SHARDS),
        P("dp", SHARDS),
        P(SHARDS, None, None),
        P(SHARDS),
        P(),
    )
    return jax.shard_map(
        per_device, mesh=mesh, in_specs=in_specs, out_specs=P(SHARDS, "dp"), check_vma=False
    )
```

time: 68.2 us -> 20.8 us (0.30)
  waiting for transfers between devices: 35 us -> 4.96 us
  blocking collectives: 15.5 us -> 0 us
  between operations: 13.4 us -> 0.05 us
  starting transfers between devices: 0.01 us -> 11.5 us
  Pallas kernels: 0 us -> 3.55 us
  matrix products: 3.12 us -> 0 us
    reduce_scatter x1 -> x0, waiting for transfers between devices: 35 us -> none  [per_device(): lax.psum_scatter(gathered, ('section', 'half'), scatter_dimension=0, tile...]
    all_gather x1 -> x0, blocking collectives: 15.5 us -> none  [per_device(): lax.all_gather(weighted, 'dp', axis=0, tiled=True)]
    ppermute x0 -> x7, starting transfers between devices: none -> 11.5 us  [the longest x3 7.86 us: per_device(): lax.ppermute(query, 'dp', [(i, (i + s) % n) for i in range(n)])]
    ppermute x0 -> x7, waiting for transfers between devices: none -> 4.96 us  [the longest x3 3.23 us: per_device(): lax.ppermute(both[s].astype(RT), 'section', [(i, i ^ s) for i in range(se...]
    pallas_call x0 -> x2, Pallas kernels: none -> 3.55 us  [the longest x1 2.17 us: per_device(): pl.pallas_call(stage, out_shape=(pltpu.VMEM(train.shape, train.dtype), pl...]
    dot_general x2 -> x0, matrix products: 3.12 us -> none  [the longest x1 1.75 us: per_device(): lax.dot_general(lax.all_gather(weighted, 'dp', axis=0, tiled=True), train...]
    reduce_sum x1 -> x0, other arithmetic: 1 us -> none  [per_device(): factor = jnp.sum(onehot * kind_scale[None, :], axis=1)]
  transfers between devices with their start and end apart: 1 -> 7, of which waited for: 1 -> 6; matrix products, arithmetic and copies ran while one was open for 0% -> 0% of each run, Pallas kernels for 0% -> 10%
where the time goes in v1:
time: 20.8 us; the launch traced here: 20.7 us
  starting transfers between devices  11.5 us (55%)
  waiting for transfers between devices  4.96 us (24%)
  Pallas kernels  3.55 us (17%)
  other arithmetic  0.65 us (3%)
    ppermute x3, starting transfers between devices, per_device(): lax.ppermute(query, 'dp', [(i, (i + s) % n) for i in range(n)])  7.86 us
    ppermute x3, starting transfers between devices, per_device(): lax.ppermute(both[s].astype(RT), 'section', [(i, i ^ s) for i in range(se...  3.55 us
    ppermute x3, waiting for transfers between devices, per_device(): lax.ppermute(both[s].astype(RT), 'section', [(i, i ^ s) for i in range(se...  3.23 us
    pallas_call x1, Pallas kernels, per_device(): pl.pallas_call(stage, out_shape=(pltpu.VMEM(train.shape, train.dtype), pl...  2.17 us
    pallas_call x1, Pallas kernels, per_device(): pl.pallas_call(functools.partial(local_scores, n, sections, halves, direc...  1.38 us
    ppermute x1, waiting for transfers between devices, per_device(): got = lax.ppermute(send, 'half', [(i, 1 - i) for i in range(halves)])  1.33 us
    add x1, other arithmetic, per_device(): out = out + moved.astype(jnp.float32)  0.62 us
  transfers between devices with their start and end apart: 7, of which 6 were waited for; matrix products, arithmetic and copies ran while one was open for 0% of the time, Pallas kernels for 10%

profile of v1, /device:TPU:0, one launch (start us, length us, event | category | flops | bytes accessed | tf_op | source)
XLA Modules:
  0.0 20.7 jit_solution(8763109723836346270)
XLA Ops:
  0.0 0.0 copy-start
  0.0 4.0 %collective-permute-start.1 = (bf16[16,1536]{1,0:T(8,128)(2,1)}, bf16[16,1536]{1,0:T(8,128)(2,1)S(1)}, u32[]{:S(2)}, u32[]{:S(2)}) collective-permute-start(bf16[16,1536]{1,0:T(8,128)(2,1)} %refs_0_.1), channel_id=1, source_target_pairs={{0,2},{1,3},{2,0},{3,1},{4,6},{5,7},{6,4},{7,5},{8,10},{9,11},{10,... | collective-permute-start | bytes 147464 | tf_op jit(solution)/shard_map/ppermute | solution.py:78
  4.0 1.6 %collective-permute-start = (bf16[16,1536]{1,0:T(8,128)(2,1)}, bf16[16,1536]{1,0:T(8,128)(2,1)S(1)}, u32[]{:S(2)}, u32[]{:S(2)}) collective-permute-start(bf16[16,1536]{1,0:T(8,128)(2,1)} %refs_0_.1), channel_id=1, source_target_pairs={{0,1},{1,2},{2,3},{3,0},{4,5},{5,6},{6,7},{7,4},{8,9},{9,10},{10,1... | collective-permute-start | bytes 147464 | tf_op jit(solution)/shard_map/ppermute | solution.py:78
  5.6 2.2 %collective-permute-start.2 = (bf16[16,1536]{1,0:T(8,128)(2,1)}, bf16[16,1536]{1,0:T(8,128)(2,1)S(1)}, u32[]{:S(2)}, u32[]{:S(2)}) collective-permute-start(bf16[16,1536]{1,0:T(8,128)(2,1)} %refs_0_.1), channel_id=1, source_target_pairs={{0,3},{1,0},{2,1},{3,2},{4,7},{5,4},{6,5},{7,6},{8,11},{9,8},{10,9... | collective-permute-start | bytes 147464 | tf_op jit(solution)/shard_map/ppermute | solution.py:78
  7.9 2.2 %stage.1 = (bf16[1024,1536]{1,0:T(8,128)(2,1)S(1)}, bf16[6,256,256]{2,1,0:T(8,128)(2,1)S(1)}, f32[6,1,256]{2,1,0:T(1,128)S(1)}) custom-call(bf16[1024,1536]{1,0:T(8,128)(2,1)} %train.1, bf16[6,256,256]{2,1,0:T(8,128)(2,1)} %precond.1, s32[6]{0:T(128)} %kind.1, f32[7]{0:T(128)} %scale.1), custom_call_target="tpu_custom_call" | custom-call | bytes 6291456 | tf_op jit(solution)/shard_map/stage/pallas_call | solution.py:83
  10.0 0.0 collective-permute-done.1.refs_2_
  10.1 0.2 collective-permute-done.refs_1_
  10.2 0.2 collective-permute-done.2.refs_3_
  10.4 0.0 copy-done
  10.4 1.4 %local_scores.1 = (f32[4,8,1024]{2,1,0:T(8,128)S(1)}, f32[4,8,1024]{2,1,0:T(8,128)S(1)}) custom-call(bf16[16,1536]{1,0:T(8,128)(2,1)S(1)} %copy-done, bf16[16,1536]{1,0:T(8,128)(2,1)S(1)} %collective-permute-done.refs_1_, bf16[16,1536]{1,0:T(8,128)(2,1)S(1)} %collective-permute-done.1.refs_2_, bf16[16,1536]{1,0:T(8,128)(2,1)S(1)} %collective-permute-done.2.refs_3_, ...), custom_call_target="tpu_custom_call" | custom-call | tf_op jit(solution)/shard_map/local_scores/pallas_call | solution.py:102
  11.8 0.1 collective-permute-start.3
  11.9 1.3 %collective-permute-done.3 = f32[4,8,1024]{2,1,0:T(8,128)S(1)} collective-permute-done((f32[4,8,1024]{2,1,0:T(8,128)S(1)}, f32[4,8,1024]{2,1,0:T(8,128)S(1)}, u32[]{:S(2)}, u32[]{:S(2)}) %collective-permute-start.3) | collective-permute-done | bytes 131104 | tf_op jit(solution)/shard_map/ppermute | solution.py:110
  13.3 1.6 %collective-permute-start.4 = (bf16[8,1024]{1,0:T(8,128)(2,1)S(1)}, bf16[8,1024]{1,0:T(8,128)(2,1)S(1)}, u32[]{:S(2)}, u32[]{:S(2)}) collective-permute-start(bf16[8,1024]{1,0:T(8,128)(2,1)S(1)} %get-tuple-element.17), channel_id=1, source_target_pairs={{0,8},{8,0},{16,24},{24,16},{1,9},{9,1},{17,25},{25,17},{2,10},{10... | collective-permute-start | bytes 49160 | tf_op jit(solution)/shard_map/ppermute | solution.py:114
  14.8 1.5 %collective-permute-start.6 = (bf16[8,1024]{1,0:T(8,128)(2,1)S(1)}, bf16[8,1024]{1,0:T(8,128)(2,1)S(1)}, u32[]{:S(2)}, u32[]{:S(2)}) collective-permute-start(bf16[8,1024]{1,0:T(8,128)(2,1)S(1)} %get-tuple-element.18), channel_id=1, source_target_pairs={{0,24},{8,16},{16,8},{24,0},{1,25},{9,17},{17,9},{25,1},{2,26},{10... | collective-permute-start | bytes 49160 | tf_op jit(solution)/shard_map/ppermute | solution.py:114
  16.3 0.5 %collective-permute-start.5 = (bf16[8,1024]{1,0:T(8,128)(2,1)S(1)}, bf16[8,1024]{1,0:T(8,128)(2,1)S(1)}, u32[]{:S(2)}, u32[]{:S(2)}) collective-permute-start(bf16[8,1024]{1,0:T(8,128)(2,1)S(1)} %get-tuple-element.19), channel_id=1, source_target_pairs={{0,16},{8,24},{16,0},{24,8},{1,17},{9,25},{17,1},{25,9},{2,18},{10... | collective-permute-start | bytes 49160 | tf_op jit(solution)/shard_map/ppermute | solution.py:114
  16.8 0.2 %collective-permute-done.4 = bf16[8,1024]{1,0:T(8,128)(2,1)S(1)} collective-permute-done((bf16[8,1024]{1,0:T(8,128)(2,1)S(1)}, bf16[8,1024]{1,0:T(8,128)(2,1)S(1)}, u32[]{:S(2)}, u32[]{:S(2)}) %collective-permute-start.4) | collective-permute-done | bytes 16416 | tf_op jit(solution)/shard_map/ppermute | solution.py:114
  17.1 2.4 %collective-permute-done.6 = bf16[8,1024]{1,0:T(8,128)(2,1)S(1)} collective-permute-done((bf16[8,1024]{1,0:T(8,128)(2,1)S(1)}, bf16[8,1024]{1,0:T(8,128)(2,1)S(1)}, u32[]{:S(2)}, u32[]{:S(2)}) %collective-permute-start.6) | collective-permute-done | bytes 16416 | tf_op jit(solution)/shard_map/ppermute | solution.py:114
  19.5 0.6 %collective-permute-done.5 = bf16[8,1024]{1,0:T(8,128)(2,1)S(1)} collective-permute-done((bf16[8,1024]{1,0:T(8,128)(2,1)S(1)}, bf16[8,1024]{1,0:T(8,128)(2,1)S(1)}, u32[]{:S(2)}, u32[]{:S(2)}) %collective-permute-start.5) | collective-permute-done | bytes 16416 | tf_op jit(solution)/shard_map/ppermute | solution.py:114
  20.1 0.6 %fusion.2 = f32[8,1024]{1,0:T(8,128)} fusion(f32[4,8,1024]{2,1,0:T(8,128)S(1)} %get-tuple-element.16, bf16[8,1024]{1,0:T(8,128)(2,1)S(1)} %collective-permute-done.6, bf16[8,1024]{1,0:T(8,128)(2,1)S(1)} %collective-permute-done.5, bf16[8,1024]{1,0:T(8,128)(2,1)S(1)} %collective-permute-done.4), kind=kLoop, calls=%fused_computation.3 | loop fusion | flops 49152 | bytes 114688 | tf_op jit(solution)/shard_map/add | solution.py:115
  (2 shorter events, 0.0 us)
Async XLA Ops:
  0.0 10.4 %copy-start = (bf16[16,1536]{1,0:T(8,128)(2,1)S(1)}, bf16[16,1536]{1,0:T(8,128)(2,1)}, u32[]{:S(2)}) copy-start(bf16[16,1536]{1,0:T(8,128)(2,1)} %refs_0_.1) | copy-start | bytes 147460
  0.0 10.0 %collective-permute-start.1 = (bf16[16,1536]{1,0:T(8,128)(2,1)}, bf16[16,1536]{1,0:T(8,128)(2,1)S(1)}, u32[]{:S(2)}, u32[]{:S(2)}) collective-permute-start(bf16[16,1536]{1,0:T(8,128)(2,1)} %refs_0_.1), channel_id=1, source_target_pairs={{0,2},{1,3},{2,0},{3,1},{4,6},{5,7},{6,4},{7,5},{8,10},{9,11},{10,... | collective-permute-start | bytes 147464 | tf_op jit(solution)/shard_map/ppermute | solution.py:78
  4.0 6.2 %collective-permute-start = (bf16[16,1536]{1,0:T(8,128)(2,1)}, bf16[16,1536]{1,0:T(8,128)(2,1)S(1)}, u32[]{:S(2)}, u32[]{:S(2)}) collective-permute-start(bf16[16,1536]{1,0:T(8,128)(2,1)} %refs_0_.1), channel_id=1, source_target_pairs={{0,1},{1,2},{2,3},{3,0},{4,5},{5,6},{6,7},{7,4},{8,9},{9,10},{10,1... | collective-permute-start | bytes 147464 | tf_op jit(solution)/shard_map/ppermute | solution.py:78
  5.6 4.8 %collective-permute-start.2 = (bf16[16,1536]{1,0:T(8,128)(2,1)}, bf16[16,1536]{1,0:T(8,128)(2,1)S(1)}, u32[]{:S(2)}, u32[]{:S(2)}) collective-permute-start(bf16[16,1536]{1,0:T(8,128)(2,1)} %refs_0_.1), channel_id=1, source_target_pairs={{0,3},{1,0},{2,1},{3,2},{4,7},{5,4},{6,5},{7,6},{8,11},{9,8},{10,9... | collective-permute-start | bytes 147464 | tf_op jit(solution)/shard_map/ppermute | solution.py:78
  11.8 1.4 %collective-permute-start.3 = (f32[4,8,1024]{2,1,0:T(8,128)S(1)}, f32[4,8,1024]{2,1,0:T(8,128)S(1)}, u32[]{:S(2)}, u32[]{:S(2)}) collective-permute-start(f32[4,8,1024]{2,1,0:T(8,128)S(1)} %get-tuple-element.14), channel_id=1, source_target_pairs={{0,4},{4,0},{1,5},{5,1},{2,6},{6,2},{3,7},{7,3},{8,12},{12,8},{9,1... | collective-permute-start | bytes 393224 | tf_op jit(solution)/shard_map/ppermute | solution.py:110
  13.3 3.8 %collective-permute-start.4 = (bf16[8,1024]{1,0:T(8,128)(2,1)S(1)}, bf16[8,1024]{1,0:T(8,128)(2,1)S(1)}, u32[]{:S(2)}, u32[]{:S(2)}) collective-permute-start(bf16[8,1024]{1,0:T(8,128)(2,1)S(1)} %get-tuple-element.17), channel_id=1, source_target_pairs={{0,8},{8,0},{16,24},{24,16},{1,9},{9,1},{17,25},{25,17},{2,10},{10... | collective-permute-start | bytes 49160 | tf_op jit(solution)/shard_map/ppermute | solution.py:114
  14.8 4.6 %collective-permute-start.6 = (bf16[8,1024]{1,0:T(8,128)(2,1)S(1)}, bf16[8,1024]{1,0:T(8,128)(2,1)S(1)}, u32[]{:S(2)}, u32[]{:S(2)}) collective-permute-start(bf16[8,1024]{1,0:T(8,128)(2,1)S(1)} %get-tuple-element.18), channel_id=1, source_target_pairs={{0,24},{8,16},{16,8},{24,0},{1,25},{9,17},{17,9},{25,1},{2,26},{10... | collective-permute-start | bytes 49160 | tf_op jit(solution)/shard_map/ppermute | solution.py:114
  16.3 3.7 %collective-permute-start.5 = (bf16[8,1024]{1,0:T(8,128)(2,1)S(1)}, bf16[8,1024]{1,0:T(8,128)(2,1)S(1)}, u32[]{:S(2)}, u32[]{:S(2)}) collective-permute-start(bf16[8,1024]{1,0:T(8,128)(2,1)S(1)} %get-tuple-element.19), channel_id=1, source_target_pairs={{0,16},{8,24},{16,0},{24,8},{1,17},{9,25},{17,1},{25,9},{2,18},{10... | collective-permute-start | bytes 49160 | tf_op jit(solution)/shard_map/ppermute | solution.py:114

commit v2 on v1

v2 whole, which is shorter than its diff:
```python
import functools

import jax
import jax.numpy as jnp
from jax import lax
from jax.experimental import pallas as pl
from jax.experimental.pallas import tpu as pltpu
from jax.sharding import PartitionSpec as P

SHARDS = ("section", "half")
DIRECT = 4
ROWS = 64
SHUFFLES = ((1, 3, 0, 2), (3, 2, 1, 0), (2, 0, 3, 1))
SENT = (1, 0, 2)
SECTION_ORDER = (1, 2, 3)


def stage(pieces, train, precond, kind, scale, train_t, precond_v, factor, raw, kind_s, scale_s, sems):
    rows = train.shape[0] // pieces
    cuts = [pl.ds(i * rows, rows) for i in range(pieces)]
    pairs = [(kind, kind_s), (scale, scale_s), (precond, precond_v)] + [(train.at[c], raw.at[c]) for c in cuts]
    copies = [pltpu.make_async_copy(src, dst, sems.at[i]) for i, (src, dst) in enumerate(pairs)]
    for c in copies:
        c.start()
    copies[0].wait()
    copies[1].wait()
    for m in range(factor.shape[0]):
        factor[m] = jnp.full(factor.shape[1:], scale_s[kind_s[m]], jnp.float32)
    for i in range(pieces):
        copies[3 + i].wait()
        train_t[:, i * rows:(i + 1) * rows] = raw[i * rows:(i + 1) * rows, :].T
    copies[2].wait()


def local_scores(n, sections, halves, direct, *refs):
    blocks, (train_t, precond, factor, kept, sent) = refs[:-5], refs[-5:]
    mods, feat = precond.shape[0], precond.shape[1]
    q_rows = blocks[0].shape[0] if direct else blocks[0].shape[0] // n
    own_rows = kept.shape[1]
    unit = min(q_rows, own_rows)
    dp, section, half = (lax.axis_index(a) for a in ("dp", "section", "half"))

    def work(lhs, rows, first_row):
        parts = []
        for m in range(mods):
            pre = jnp.dot(lhs(slice(m * feat, (m + 1) * feat)), precond[m], preferred_element_type=jnp.float32)
            parts.append((pre * factor[m]).astype(jnp.bfloat16))
        scores = jnp.dot(jnp.concatenate(parts, axis=1), train_t[...], preferred_element_type=jnp.float32)
        for i in range(rows // unit):
            row = first_row(i * unit)
            device, at = row // own_rows, pl.multiple_of(lax.rem(row, own_rows), unit)
            slot, mine = (device // halves) ^ section, lax.rem(device, halves) == half
            value = scores[i * unit:(i + 1) * unit]

            @pl.when(mine)
            def _():
                kept[slot, pl.ds(at, unit), :] = value

            @pl.when(jnp.logical_not(mine))
            def _():
                sent[slot, pl.ds(at, unit), :] = value.astype(sent.dtype)

    if direct:
        owners = [dp]
        for k in SENT:
            table = {t: i for i, t in enumerate(SHUFFLES[k])}
            owner = jnp.int32(table[0])
            for t in range(1, n):
                owner = jnp.where(dp == t, table[t], owner)
            owners.append(owner)
        work(lambda c: jnp.concatenate([b[:, c] for b in blocks], axis=0), n * q_rows, lambda r: owners[r // q_rows] * q_rows + r % q_rows)
    else:

        def step(c, carry):
            base = pl.multiple_of(c * ROWS, ROWS)
            work(lambda cols: blocks[0][pl.ds(base, ROWS), cols], ROWS, lambda r: base + r)
            return carry

        lax.fori_loop(0, n * q_rows // ROWS, step, 0)


def per_device(query, train, precond, module_kind, kind_scale):
    n, sections, halves = (lax.axis_size(a) for a in ("dp", "section", "half"))
    mods, feat = precond.shape[:2]
    cols, feats = train.shape
    own_rows = n * query.shape[0] // (sections * halves)
    direct = n == DIRECT
    if direct:
        blocks = [query] + [lax.ppermute(query, "dp", list(enumerate(SHUFFLES[k]))) for k in SENT]
    else:
        blocks = [lax.all_gather(query, "dp", axis=0, tiled=True)]

    vmem, hbm = (pl.BlockSpec(memory_space=s) for s in (pltpu.VMEM, pltpu.HBM))
    pieces = 4
    staged = pl.pallas_call(
        functools.partial(stage, pieces),
        out_shape=(
            pltpu.VMEM((feats, cols), train.dtype),
            pltpu.VMEM(precond.shape, precond.dtype),
            pltpu.VMEM((mods, 1, feat), jnp.float32),
        ),
        in_specs=[hbm] * 4,
        out_specs=(vmem,) * 3,
        scratch_shapes=[
            pltpu.VMEM(train.shape, train.dtype),
            pltpu.SMEM(module_kind.shape, module_kind.dtype),
            pltpu.SMEM(kind_scale.shape, kind_scale.dtype),
            pltpu.SemaphoreType.DMA((3 + pieces,)),
        ],
        cost_estimate=pl.CostEstimate(flops=0, bytes_accessed=4 * train.size, transcendentals=0),
        compiler_params=pltpu.CompilerParams(vmem_limit_bytes=32 * 2**20),
        name="stage",
    )(*(pltpu.with_memory_space_constraint(a, pltpu.HBM) for a in (train, precond, module_kind, kind_scale)))
    shape = (sections, own_rows, cols)
    kept, sent = pl.pallas_call(
        functools.partial(local_scores, n, sections, halves, direct),
        out_shape=(jax.ShapeDtypeStruct(shape, jnp.float32), jax.ShapeDtypeStruct(shape, jnp.float32)),
        in_specs=[vmem] * (len(blocks) + 3),
        out_specs=(vmem, vmem),
        compiler_params=pltpu.CompilerParams(vmem_limit_bytes=48 * 2**20),
        name="local_scores",
    )(*blocks, *staged)

    got = lax.ppermute(sent, "half", [(i, halves - 1 - i) for i in range(halves)])
    total = kept + got.astype(jnp.float32)
    out = total[0]
    for s in SECTION_ORDER if sections == 4 else range(1, sections):
        moved = lax.ppermute(total[s].astype(jnp.bfloat16), "section", [(i, i ^ s) for i in range(sections)])
        out = out + moved.astype(jnp.float32)
    return out


def solution(mesh):
    in_specs = (
        P("dp", SHARDS),
        P("dp", SHARDS),
        P(SHARDS, None, None),
        P(SHARDS),
        P(),
    )
    return jax.shard_map(
        per_device, mesh=mesh, in_specs=in_specs, out_specs=P(SHARDS, "dp"), check_vma=False
    )
```

time: 20.8 us -> 19.9 us (0.957)
  starting transfers between devices: 11.5 us -> 10.7 us
    ppermute x7, starting transfers between devices: 11.5 us -> 10.7 us  [the longest x3 7.07 us: per_device(): lax.ppermute(query, 'dp', list(enumerate(SHUFFLES[k])))]
    pallas_call x1, Pallas kernels: 1.38 us -> 0.94 us  [per_device(): pl.pallas_call(functools.partial(local_scores, n, sections, halves, direc...]
    pallas_call x1, Pallas kernels: 2.17 us -> 2.53 us  [per_device(): pl.pallas_call(functools.partial(stage, pieces), out_shape=(pltpu.VMEM((f...]
  transfers between devices with their start and end apart: 7 -> 7, of which waited for: 6 -> 5; matrix products, arithmetic and copies ran while one was open for 0% -> 0% of each run, Pallas kernels for 10% -> 13%
where the time goes in v2:
time: 19.9 us; the launch traced here: 19.8 us
  starting transfers between devices  10.7 us (54%)
  waiting for transfers between devices  4.87 us (24%)
  Pallas kernels  3.47 us (17%)
  other arithmetic  0.65 us (3%)
    ppermute x3, starting transfers between devices, per_device(): lax.ppermute(query, 'dp', list(enumerate(SHUFFLES[k])))  7.07 us
    ppermute x3, starting transfers between devices, per_device(): lax.ppermute(total[s].astype(jnp.bfloat16), 'section', [(i, i ^ s) for i...  3.55 us
    ppermute x3, waiting for transfers between devices, per_device(): lax.ppermute(total[s].astype(jnp.bfloat16), 'section', [(i, i ^ s) for i...  3.23 us
    pallas_call x1, Pallas kernels, per_device(): pl.pallas_call(functools.partial(stage, pieces), out_shape=(pltpu.VMEM((f...  2.53 us
    ppermute x1, waiting for transfers between devices, per_device(): lax.ppermute(sent, 'half', [(i, halves - 1 - i) for i in range(halves)])  1.33 us
    pallas_call x1, Pallas kernels, per_device(): pl.pallas_call(functools.partial(local_scores, n, sections, halves, direc...  0.94 us
    add x1, other arithmetic, per_device(): out = out + moved.astype(jnp.float32)  0.62 us
  transfers between devices with their start and end apart: 7, of which 5 were waited for; matrix products, arithmetic and copies ran while one was open for 0% of the time, Pallas kernels for 13%

profile of v2, /device:TPU:0, one launch (start us, length us, event | category | flops | bytes accessed | tf_op | source)
XLA Modules:
  0.0 19.8 jit_solution(8499467133817073182)
XLA Ops:
  0.0 0.0 copy-start
  0.0 3.0 %collective-permute-start.1 = (bf16[16,1536]{1,0:T(8,128)(2,1)}, bf16[16,1536]{1,0:T(8,128)(2,1)S(1)}, u32[]{:S(2)}, u32[]{:S(2)}) collective-permute-start(bf16[16,1536]{1,0:T(8,128)(2,1)} %refs_0_.1), channel_id=1, source_target_pairs={{0,1},{1,3},{2,0},{3,2},{4,5},{5,7},{6,4},{7,6},{8,9},{9,11},{10,8... | collective-permute-start | bytes 147464 | tf_op jit(solution)/shard_map/ppermute | solution.py:89
  3.0 2.5 %collective-permute-start = (bf16[16,1536]{1,0:T(8,128)(2,1)}, bf16[16,1536]{1,0:T(8,128)(2,1)S(1)}, u32[]{:S(2)}, u32[]{:S(2)}) collective-permute-start(bf16[16,1536]{1,0:T(8,128)(2,1)} %refs_0_.1), channel_id=1, source_target_pairs={{0,3},{1,2},{2,1},{3,0},{4,7},{5,6},{6,5},{7,4},{8,11},{9,10},{10,... | collective-permute-start | bytes 147464 | tf_op jit(solution)/shard_map/ppermute | solution.py:89
  5.5 1.6 %collective-permute-start.2 = (bf16[16,1536]{1,0:T(8,128)(2,1)}, bf16[16,1536]{1,0:T(8,128)(2,1)S(1)}, u32[]{:S(2)}, u32[]{:S(2)}) collective-permute-start(bf16[16,1536]{1,0:T(8,128)(2,1)} %refs_0_.1), channel_id=1, source_target_pairs={{0,2},{1,0},{2,3},{3,1},{4,6},{5,4},{6,7},{7,5},{8,10},{9,8},{10,1... | collective-permute-start | bytes 147464 | tf_op jit(solution)/shard_map/ppermute | solution.py:89
  7.1 2.5 %stage.1 = (bf16[1536,1024]{1,0:T(8,128)(2,1)S(1)}, bf16[6,256,256]{2,1,0:T(8,128)(2,1)S(1)}, f32[6,1,256]{2,1,0:T(1,128)S(1)}) custom-call(bf16[1024,1536]{1,0:T(8,128)(2,1)} %train.1, bf16[6,256,256]{2,1,0:T(8,128)(2,1)} %precond.1, s32[6]{0:T(128)} %kind.1, f32[7]{0:T(128)} %scale.1), custom_call_target="tpu_custom_call" | custom-call | bytes 6291456 | tf_op jit(solution)/shard_map/stage/pallas_call | solution.py:95
  9.6 0.0 collective-permute-done.1.refs_2_
  9.6 0.0 collective-permute-done.refs_1_
  9.6 0.3 %collective-permute-done.2.refs_3_ = bf16[16,1536]{1,0:T(8,128)(2,1)S(1)} collective-permute-done((bf16[16,1536]{1,0:T(8,128)(2,1)}, bf16[16,1536]{1,0:T(8,128)(2,1)S(1)}, u32[]{:S(2)}, u32[]{:S(2)}) %collective-permute-start.2) | collective-permute-done | bytes 49184 | tf_op jit(solution)/shard_map/ppermute | solution.py:89
  9.9 0.0 copy-done
  9.9 0.9 %local_scores.1 = (f32[4,8,1024]{2,1,0:T(8,128)S(1)}, f32[4,8,1024]{2,1,0:T(8,128)S(1)}) custom-call(bf16[16,1536]{1,0:T(8,128)(2,1)S(1)} %copy-done, bf16[16,1536]{1,0:T(8,128)(2,1)S(1)} %collective-permute-done.refs_1_, bf16[16,1536]{1,0:T(8,128)(2,1)S(1)} %collective-permute-done.1.refs_2_, bf16[16,1536]{1,0:T(8,128)(2,1)S(1)} %collective-permute-done.2.refs_3_, ...), custom_call_target="tpu_custom_call" | custom-call | tf_op jit(solution)/shard_map/local_scores/pallas_call | solution.py:115
  10.9 0.1 collective-permute-start.3
  11.0 1.3 %collective-permute-done.3 = f32[4,8,1024]{2,1,0:T(8,128)S(1)} collective-permute-done((f32[4,8,1024]{2,1,0:T(8,128)S(1)}, f32[4,8,1024]{2,1,0:T(8,128)S(1)}, u32[]{:S(2)}, u32[]{:S(2)}) %collective-permute-start.3) | collective-permute-done | bytes 131104 | tf_op jit(solution)/shard_map/ppermute | solution.py:124
  12.3 1.6 %collective-permute-start.4 = (bf16[8,1024]{1,0:T(8,128)(2,1)S(1)}, bf16[8,1024]{1,0:T(8,128)(2,1)S(1)}, u32[]{:S(2)}, u32[]{:S(2)}) collective-permute-start(bf16[8,1024]{1,0:T(8,128)(2,1)S(1)} %get-tuple-element.17), channel_id=1, source_target_pairs={{0,8},{8,0},{16,24},{24,16},{1,9},{9,1},{17,25},{25,17},{2,10},{10... | collective-permute-start | bytes 49160 | tf_op jit(solution)/shard_map/ppermute | solution.py:128
  13.9 1.5 %collective-permute-start.6 = (bf16[8,1024]{1,0:T(8,128)(2,1)S(1)}, bf16[8,1024]{1,0:T(8,128)(2,1)S(1)}, u32[]{:S(2)}, u32[]{:S(2)}) collective-permute-start(bf16[8,1024]{1,0:T(8,128)(2,1)S(1)} %get-tuple-element.18), channel_id=1, source_target_pairs={{0,24},{8,16},{16,8},{24,0},{1,25},{9,17},{17,9},{25,1},{2,26},{10... | collective-permute-start | bytes 49160 | tf_op jit(solution)/shard_map/ppermute | solution.py:128
  15.4 0.5 %collective-permute-start.5 = (bf16[8,1024]{1,0:T(8,128)(2,1)S(1)}, bf16[8,1024]{1,0:T(8,128)(2,1)S(1)}, u32[]{:S(2)}, u32[]{:S(2)}) collective-permute-start(bf16[8,1024]{1,0:T(8,128)(2,1)S(1)} %get-tuple-element.19), channel_id=1, source_target_pairs={{0,16},{8,24},{16,0},{24,8},{1,17},{9,25},{17,1},{25,9},{2,18},{10... | collective-permute-start | bytes 49160 | tf_op jit(solution)/shard_map/ppermute | solution.py:128
  15.9 0.2 %collective-permute-done.4 = bf16[8,1024]{1,0:T(8,128)(2,1)S(1)} collective-permute-done((bf16[8,1024]{1,0:T(8,128)(2,1)S(1)}, bf16[8,1024]{1,0:T(8,128)(2,1)S(1)}, u32[]{:S(2)}, u32[]{:S(2)}) %collective-permute-start.4) | collective-permute-done | bytes 16416 | tf_op jit(solution)/shard_map/ppermute | solution.py:128
  16.1 2.4 %collective-permute-done.6 = bf16[8,1024]{1,0:T(8,128)(2,1)S(1)} collective-permute-done((bf16[8,1024]{1,0:T(8,128)(2,1)S(1)}, bf16[8,1024]{1,0:T(8,128)(2,1)S(1)}, u32[]{:S(2)}, u32[]{:S(2)}) %collective-permute-start.6) | collective-permute-done | bytes 16416 | tf_op jit(solution)/shard_map/ppermute | solution.py:128
  18.5 0.6 %collective-permute-done.5 = bf16[8,1024]{1,0:T(8,128)(2,1)S(1)} collective-permute-done((bf16[8,1024]{1,0:T(8,128)(2,1)S(1)}, bf16[8,1024]{1,0:T(8,128)(2,1)S(1)}, u32[]{:S(2)}, u32[]{:S(2)}) %collective-permute-start.5) | collective-permute-done | bytes 16416 | tf_op jit(solution)/shard_map/ppermute | solution.py:128
  19.1 0.6 %fusion.2 = f32[8,1024]{1,0:T(8,128)} fusion(f32[4,8,1024]{2,1,0:T(8,128)S(1)} %get-tuple-element.16, bf16[8,1024]{1,0:T(8,128)(2,1)S(1)} %collective-permute-done.6, bf16[8,1024]{1,0:T(8,128)(2,1)S(1)} %collective-permute-done.5, bf16[8,1024]{1,0:T(8,128)(2,1)S(1)} %collective-permute-done.4), kind=kLoop, calls=%fused_computation.3 | loop fusion | flops 49152 | bytes 114688 | tf_op jit(solution)/shard_map/add | solution.py:129
  (2 shorter events, 0.0 us)
Async XLA Ops:
  0.0 9.9 %copy-start = (bf16[16,1536]{1,0:T(8,128)(2,1)S(1)}, bf16[16,1536]{1,0:T(8,128)(2,1)}, u32[]{:S(2)}) copy-start(bf16[16,1536]{1,0:T(8,128)(2,1)} %refs_0_.1) | copy-start | bytes 147460
  0.0 9.6 %collective-permute-start.1 = (bf16[16,1536]{1,0:T(8,128)(2,1)}, bf16[16,1536]{1,0:T(8,128)(2,1)S(1)}, u32[]{:S(2)}, u32[]{:S(2)}) collective-permute-start(bf16[16,1536]{1,0:T(8,128)(2,1)} %refs_0_.1), channel_id=1, source_target_pairs={{0,1},{1,3},{2,0},{3,2},{4,5},{5,7},{6,4},{7,6},{8,9},{9,11},{10,8... | collective-permute-start | bytes 147464 | tf_op jit(solution)/shard_map/ppermute | solution.py:89
  3.0 6.6 %collective-permute-start = (bf16[16,1536]{1,0:T(8,128)(2,1)}, bf16[16,1536]{1,0:T(8,128)(2,1)S(1)}, u32[]{:S(2)}, u32[]{:S(2)}) collective-permute-start(bf16[16,1536]{1,0:T(8,128)(2,1)} %refs_0_.1), channel_id=1, source_target_pairs={{0,3},{1,2},{2,1},{3,0},{4,7},{5,6},{6,5},{7,4},{8,11},{9,10},{10,... | collective-permute-start | bytes 147464 | tf_op jit(solution)/shard_map/ppermute | solution.py:89
  5.5 4.4 %collective-permute-start.2 = (bf16[16,1536]{1,0:T(8,128)(2,1)}, bf16[16,1536]{1,0:T(8,128)(2,1)S(1)}, u32[]{:S(2)}, u32[]{:S(2)}) collective-permute-start(bf16[16,1536]{1,0:T(8,128)(2,1)} %refs_0_.1), channel_id=1, source_target_pairs={{0,2},{1,0},{2,3},{3,1},{4,6},{5,4},{6,7},{7,5},{8,10},{9,8},{10,1... | collective-permute-start | bytes 147464 | tf_op jit(solution)/shard_map/ppermute | solution.py:89
  10.9 1.4 %collective-permute-start.3 = (f32[4,8,1024]{2,1,0:T(8,128)S(1)}, f32[4,8,1024]{2,1,0:T(8,128)S(1)}, u32[]{:S(2)}, u32[]{:S(2)}) collective-permute-start(f32[4,8,1024]{2,1,0:T(8,128)S(1)} %get-tuple-element.14), channel_id=1, source_target_pairs={{0,4},{4,0},{1,5},{5,1},{2,6},{6,2},{3,7},{7,3},{8,12},{12,8},{9,1... | collective-permute-start | bytes 393224 | tf_op jit(solution)/shard_map/ppermute | solution.py:124
  12.3 3.8 %collective-permute-start.4 = (bf16[8,1024]{1,0:T(8,128)(2,1)S(1)}, bf16[8,1024]{1,0:T(8,128)(2,1)S(1)}, u32[]{:S(2)}, u32[]{:S(2)}) collective-permute-start(bf16[8,1024]{1,0:T(8,128)(2,1)S(1)} %get-tuple-element.17), channel_id=1, source_target_pairs={{0,8},{8,0},{16,24},{24,16},{1,9},{9,1},{17,25},{25,17},{2,10},{10... | collective-permute-start | bytes 49160 | tf_op jit(solution)/shard_map/ppermute | solution.py:128
  13.9 4.6 %collective-permute-start.6 = (bf16[8,1024]{1,0:T(8,128)(2,1)S(1)}, bf16[8,1024]{1,0:T(8,128)(2,1)S(1)}, u32[]{:S(2)}, u32[]{:S(2)}) collective-permute-start(bf16[8,1024]{1,0:T(8,128)(2,1)S(1)} %get-tuple-element.18), channel_id=1, source_target_pairs={{0,24},{8,16},{16,8},{24,0},{1,25},{9,17},{17,9},{25,1},{2,26},{10... | collective-permute-start | bytes 49160 | tf_op jit(solution)/shard_map/ppermute | solution.py:128
  15.4 3.7 %collective-permute-start.5 = (bf16[8,1024]{1,0:T(8,128)(2,1)S(1)}, bf16[8,1024]{1,0:T(8,128)(2,1)S(1)}, u32[]{:S(2)}, u32[]{:S(2)}) collective-permute-start(bf16[8,1024]{1,0:T(8,128)(2,1)S(1)} %get-tuple-element.19), channel_id=1, source_target_pairs={{0,16},{8,24},{16,0},{24,8},{1,17},{9,25},{17,1},{25,9},{2,18},{10... | collective-permute-start | bytes 49160 | tf_op jit(solution)/shard_map/ppermute | solution.py:128

commit v3 on v2

--- a/solution.py
+++ b/solution.py
@@ -10,9 +10,8 @@
 SHARDS = ("section", "half")
 DIRECT = 4
 ROWS = 64
-SHUFFLES = ((1, 3, 0, 2), (3, 2, 1, 0), (2, 0, 3, 1))
-SENT = (1, 0, 2)
-SECTION_ORDER = (1, 2, 3)
+SHUFFLES = ((2, 3, 1, 0), (3, 2, 0, 1), (1, 0, 3, 2))
+NEAR = (1, 3)
 
 
 def stage(pieces, train, precond, kind, scale, train_t, precond_v, factor, raw, kind_s, scale_s, sems):
@@ -32,13 +31,15 @@
     copies[2].wait()
 
 
-def local_scores(n, sections, halves, direct, *refs):
-    blocks, (train_t, precond, factor, kept, sent) = refs[:-5], refs[-5:]
+def local_scores(n, direct, *refs, far):
+    blocks, (train_t, precond, factor), outs = refs[:-6 - len(far)], refs[-6 - len(far):-3 - len(far)], refs[-3 - len(far):]
+    own, near, swap, aways = outs[0], outs[1], outs[2], outs[3:]
     mods, feat = precond.shape[0], precond.shape[1]
     q_rows = blocks[0].shape[0] if direct else blocks[0].shape[0] // n
-    own_rows = kept.shape[1]
+    own_rows = own.shape[0]
     unit = min(q_rows, own_rows)
     dp, section, half = (lax.axis_index(a) for a in ("dp", "section", "half"))
+    routes = [(0, own), (jnp.where(half == 0, *NEAR), near), (jnp.where(half == 0, *NEAR[::-1]), swap)] + list(zip(far, aways))
 
     def work(lhs, rows, first_row):
         parts = []
@@ -48,26 +49,18 @@
         scores = jnp.dot(jnp.concatenate(parts, axis=1), train_t[...], preferred_element_type=jnp.float32)
         for i in range(rows // unit):
             row = first_row(i * unit)
-            device, at = row // own_rows, pl.multiple_of(lax.rem(row, own_rows), unit)
-            slot, mine = (device // halves) ^ section, lax.rem(device, halves) == half
+            away, at = (row // own_rows) ^ section, pl.multiple_of(lax.rem(row, own_rows), unit)
             value = scores[i * unit:(i + 1) * unit]
+            for distance, out in routes:
 
-            @pl.when(mine)
-            def _():
-                kept[slot, pl.ds(at, unit), :] = value
-
-            @pl.when(jnp.logical_not(mine))
-            def _():
-                sent[slot, pl.ds(at, unit), :] = value.astype(sent.dtype)
+                @pl.when(away == distance)
+                def _(out=out):
+                    out[pl.ds(at, unit), :] = value.astype(out.dtype)
 
     if direct:
         owners = [dp]
-        for k in SENT:
-            table = {t: i for i, t in enumerate(SHUFFLES[k])}
-            owner = jnp.int32(table[0])
-            for t in range(1, n):
-                owner = jnp.where(dp == t, table[t], owner)
-            owners.append(owner)
+        for shuffle in SHUFFLES:
+            owners.append(sum(jnp.where(dp == target, source, 0) for source, target in enumerate(shuffle)))
         work(lambda c: jnp.concatenate([b[:, c] for b in blocks], axis=0), n * q_rows, lambda r: owners[r // q_rows] * q_rows + r % q_rows)
     else:
 
@@ -80,13 +73,13 @@
 
 
 def per_device(query, train, precond, module_kind, kind_scale):
-    n, sections, halves = (lax.axis_size(a) for a in ("dp", "section", "half"))
+    n, sections = lax.axis_size("dp"), lax.axis_size("section")
     mods, feat = precond.shape[:2]
     cols, feats = train.shape
-    own_rows = n * query.shape[0] // (sections * halves)
+    own_rows = n * query.shape[0] // sections
     direct = n == DIRECT
     if direct:
-        blocks = [query] + [lax.ppermute(query, "dp", list(enumerate(SHUFFLES[k]))) for k in SENT]
+        blocks = [query] + [lax.ppermute(query, "dp", list(enumerate(s))) for s in SHUFFLES]
     else:
         blocks = [lax.all_gather(query, "dp", axis=0, tiled=True)]
 
@@ -111,23 +104,30 @@
         compiler_params=pltpu.CompilerParams(vmem_limit_bytes=32 * 2**20),
         name="stage",
     )(*(pltpu.with_memory_space_constraint(a, pltpu.HBM) for a in (train, precond, module_kind, kind_scale)))
-    shape = (sections, own_rows, cols)
-    kept, sent = pl.pallas_call(
-        functools.partial(local_scores, n, sections, halves, direct),
-        out_shape=(jax.ShapeDtypeStruct(shape, jnp.float32), jax.ShapeDtypeStruct(shape, jnp.float32)),
+    far = tuple(s for s in range(1, sections) if s not in NEAR)
+    shape = (own_rows, cols)
+    whole, half_width = jax.ShapeDtypeStruct(shape, jnp.float32), jax.ShapeDtypeStruct(shape, jnp.bfloat16)
+    own, near, swap, *aways = pl.pallas_call(
+        functools.partial(local_scores, n, direct, far=far),
+        out_shape=(whole, whole, whole) + (half_width,) * len(far),
         in_specs=[vmem] * (len(blocks) + 3),
-        out_specs=(vmem, vmem),
+        out_specs=(vmem,) * (3 + len(far)),
         compiler_params=pltpu.CompilerParams(vmem_limit_bytes=48 * 2**20),
         name="local_scores",
     )(*blocks, *staged)
 
-    got = lax.ppermute(sent, "half", [(i, halves - 1 - i) for i in range(halves)])
-    total = kept + got.astype(jnp.float32)
-    out = total[0]
-    for s in SECTION_ORDER if sections == 4 else range(1, sections):
-        moved = lax.ppermute(total[s].astype(jnp.bfloat16), "section", [(i, i ^ s) for i in range(sections)])
-        out = out + moved.astype(jnp.float32)
-    return out
+    def across(x):
+        return lax.ppermute(x, "half", [(0, 1), (1, 0)])
+
+    near = (near + across(swap)).astype(jnp.bfloat16)
+    for s, away in zip(far, aways):
+        own = own + lax.ppermute(away, "section", [(i, i ^ s) for i in range(sections)]).astype(jnp.float32)
+    pairs = [(2 * i + h, 2 * (i ^ NEAR[h]) + h) for i in range(sections) for h in range(2)]
+    own = own + lax.ppermute(near, SHARDS, pairs).astype(jnp.float32)
+    rows = own_rows // 2
+    first = lax.axis_index("half") == 0
+    mine = jnp.where(first, own[:rows], own[rows:])
+    return mine + across(jnp.where(first, own[rows:], own[:rows]))
 
 
 def solution(mesh):

time: 19.9 us -> 18.7 us (0.940)
  starting transfers between devices: 10.7 us -> 8.9 us
  waiting for transfers between devices: 4.87 us -> 5.49 us
    ppermute x7, starting transfers between devices: 10.7 us -> 8.9 us  [the longest x3 5.62 us: per_device(): lax.ppermute(query, 'dp', list(enumerate(s)))]
    ppermute x7, waiting for transfers between devices: 4.87 us -> 5.49 us  [the longest x1 1.75 us: per_device(): own = own + lax.ppermute(near, SHARDS, pairs).astype(jnp.float32)]
    add x1 -> x2, other arithmetic: 0.62 us -> 0.63 us  [the longest x1 0.62 us: per_device(): return mine + across(jnp.where(first, own[rows:], own[:rows]))]
  transfers between devices with their start and end apart: 7 -> 7, of which waited for: 5 -> 5; matrix products, arithmetic and copies ran while one was open for 0% -> 0% of each run, Pallas kernels for 13% -> 14%
where the time goes in v3:
time: 18.7 us; the launch traced here: 18.5 us
  starting transfers between devices  8.9 us (48%)
  waiting for transfers between devices  5.49 us (29%)
  Pallas kernels  3.43 us (18%)
  other arithmetic  0.65 us (3%)
    ppermute x3, starting transfers between devices, per_device(): lax.ppermute(query, 'dp', list(enumerate(s)))  5.62 us
    pallas_call x1, Pallas kernels, per_device(): pl.pallas_call(functools.partial(stage, pieces), out_shape=(pltpu.VMEM((f...  2.53 us
    ppermute x1, waiting for transfers between devices, per_device(): own = own + lax.ppermute(near, SHARDS, pairs).astype(jnp.float32)  1.75 us
    ppermute x3, waiting for transfers between devices, per_device(): lax.ppermute(query, 'dp', list(enumerate(s)))  1.72 us
    ppermute x1, starting transfers between devices, per_device(): lax.ppermute(away, 'section', [(i, i ^ s) for i in range(sections)])  1.59 us
    ppermute x1, starting transfers between devices, per_device(): own = own + lax.ppermute(near, SHARDS, pairs).astype(jnp.float32)  1.56 us
    ppermute x2, waiting for transfers between devices, across(): return lax.ppermute(x, 'half', [(0, 1), (1, 0)])  1.2 us
    pallas_call x1, Pallas kernels, per_device(): pl.pallas_call(functools.partial(local_scores, n, direct, far=far), out_s...  0.9 us
  transfers between devices with their start and end apart: 7, of which 5 were waited for; matrix products, arithmetic and copies ran while one was open for 0% of the time, Pallas kernels for 14%

profile of v3, /device:TPU:0, one launch (start us, length us, event | category | flops | bytes accessed | tf_op | source)
XLA Modules:
  0.0 18.5 jit_solution(15675498542114683719)
XLA Ops:
  0.0 0.0 copy-start
  0.0 4.0 %collective-permute-start = (bf16[16,1536]{1,0:T(8,128)(2,1)}, bf16[16,1536]{1,0:T(8,128)(2,1)S(1)}, u32[]{:S(2)}, u32[]{:S(2)}) collective-permute-start(bf16[16,1536]{1,0:T(8,128)(2,1)} %refs_0_.1), channel_id=1, source_target_pairs={{0,2},{1,3},{2,1},{3,0},{4,6},{5,7},{6,5},{7,4},{8,10},{9,11},{10,... | collective-permute-start | bytes 147464 | tf_op jit(solution)/shard_map/ppermute | solution.py:82
  4.0 1.1 %collective-permute-start.1 = (bf16[16,1536]{1,0:T(8,128)(2,1)}, bf16[16,1536]{1,0:T(8,128)(2,1)S(1)}, u32[]{:S(2)}, u32[]{:S(2)}) collective-permute-start(bf16[16,1536]{1,0:T(8,128)(2,1)} %refs_0_.1), channel_id=1, source_target_pairs={{0,3},{1,2},{2,0},{3,1},{4,7},{5,6},{6,4},{7,5},{8,11},{9,10},{10,... | collective-permute-start | bytes 147464 | tf_op jit(solution)/shard_map/ppermute | solution.py:82
  5.1 0.5 %collective-permute-start.2 = (bf16[16,1536]{1,0:T(8,128)(2,1)}, bf16[16,1536]{1,0:T(8,128)(2,1)S(1)}, u32[]{:S(2)}, u32[]{:S(2)}) collective-permute-start(bf16[16,1536]{1,0:T(8,128)(2,1)} %refs_0_.1), channel_id=1, source_target_pairs={{0,1},{1,0},{2,3},{3,2},{4,5},{5,4},{6,7},{7,6},{8,9},{9,8},{10,11... | collective-permute-start | bytes 147464 | tf_op jit(solution)/shard_map/ppermute | solution.py:82
  5.6 2.5 %stage.1 = (bf16[1536,1024]{1,0:T(8,128)(2,1)S(1)}, bf16[6,256,256]{2,1,0:T(8,128)(2,1)S(1)}, f32[6,1,256]{2,1,0:T(1,128)S(1)}) custom-call(bf16[1024,1536]{1,0:T(8,128)(2,1)} %train.1, bf16[6,256,256]{2,1,0:T(8,128)(2,1)} %precond.1, s32[6]{0:T(128)} %kind.1, f32[7]{0:T(128)} %scale.1), custom_call_target="tpu_custom_call" | custom-call | bytes 6291456 | tf_op jit(solution)/shard_map/stage/pallas_call | solution.py:88
  8.2 0.0 collective-permute-done.refs_1_
  8.2 1.2 %collective-permute-done.1.refs_2_ = bf16[16,1536]{1,0:T(8,128)(2,1)S(1)} collective-permute-done((bf16[16,1536]{1,0:T(8,128)(2,1)}, bf16[16,1536]{1,0:T(8,128)(2,1)S(1)}, u32[]{:S(2)}, u32[]{:S(2)}) %collective-permute-start.1) | collective-permute-done | bytes 49184 | tf_op jit(solution)/shard_map/ppermute | solution.py:82
  9.4 0.5 %collective-permute-done.2.refs_3_ = bf16[16,1536]{1,0:T(8,128)(2,1)S(1)} collective-permute-done((bf16[16,1536]{1,0:T(8,128)(2,1)}, bf16[16,1536]{1,0:T(8,128)(2,1)S(1)}, u32[]{:S(2)}, u32[]{:S(2)}) %collective-permute-start.2) | collective-permute-done | bytes 49184 | tf_op jit(solution)/shard_map/ppermute | solution.py:82
  9.9 0.0 copy-done
  9.9 0.9 %local_scores.1 = (f32[16,1024]{1,0:T(8,128)S(1)}, f32[16,1024]{1,0:T(8,128)S(1)}, f32[16,1024]{1,0:T(8,128)S(1)}, bf16[16,1024]{1,0:T(8,128)(2,1)S(1)}) custom-call(bf16[16,1536]{1,0:T(8,128)(2,1)S(1)} %copy-done, bf16[16,1536]{1,0:T(8,128)(2,1)S(1)} %collective-permute-done.refs_1_, bf16[16,1536]{1,0:T(8,128)(2,1)S(1)} %collective-permute-done.1.refs_2_, ...), custom_call_target="tpu_custom_call" | custom-call | tf_op jit(solution)/shard_map/local_scores/pallas_call | solution.py:110
  10.8 0.1 collective-permute-start.4
  10.9 1.6 %collective-permute-start.3 = (bf16[16,1024]{1,0:T(8,128)(2,1)S(1)}, bf16[16,1024]{1,0:T(8,128)(2,1)S(1)}, u32[]{:S(2)}, u32[]{:S(2)}) collective-permute-start(bf16[16,1024]{1,0:T(8,128)(2,1)S(1)} %get-tuple-element.16), channel_id=1, source_target_pairs={{0,16},{8,24},{16,0},{24,8},{1,17},{9,25},{17,1},{25,9},{2,18},{10... | collective-permute-start | bytes 98312 | tf_op jit(solution)/shard_map/ppermute | solution.py:124
  12.5 0.0 collective-permute-done.4
  12.5 1.6 %collective-permute-start.5 = (bf16[16,1024]{1,0:T(8,128)(2,1)S(1)}, bf16[16,1024]{1,0:T(8,128)(2,1)S(1)}, u32[]{:S(2)}, u32[]{:S(2)}) collective-permute-start(bf16[16,1024]{1,0:T(8,128)(2,1)S(1)} %add_convert_fusion), channel_id=1, source_target_pairs={{0,8},{4,28},{8,0},{12,20},{16,24},{20,12},{24,16},{28,4},{1,9},{5... | collective-permute-start | bytes 98312 | tf_op jit(solution)/shard_map/ppermute | solution.py:126
  14.0 0.8 %collective-permute-done.3 = bf16[16,1024]{1,0:T(8,128)(2,1)S(1)} collective-permute-done((bf16[16,1024]{1,0:T(8,128)(2,1)S(1)}, bf16[16,1024]{1,0:T(8,128)(2,1)S(1)}, u32[]{:S(2)}, u32[]{:S(2)}) %collective-permute-start.3) | collective-permute-done | bytes 32800 | tf_op jit(solution)/shard_map/ppermute | solution.py:124
  14.9 1.8 %collective-permute-done.5 = bf16[16,1024]{1,0:T(8,128)(2,1)S(1)} collective-permute-done((bf16[16,1024]{1,0:T(8,128)(2,1)S(1)}, bf16[16,1024]{1,0:T(8,128)(2,1)S(1)}, u32[]{:S(2)}, u32[]{:S(2)}) %collective-permute-start.5) | collective-permute-done | bytes 32800 | tf_op jit(solution)/shard_map/ppermute | solution.py:126
  16.6 0.1 collective-permute-start.6
  16.7 1.2 %collective-permute-done.6 = f32[8,1024]{1,0:T(8,128)S(1)} collective-permute-done((f32[8,1024]{1,0:T(8,128)S(1)}, f32[8,1024]{1,0:T(8,128)S(1)}, u32[]{:S(2)}, u32[]{:S(2)}) %collective-permute-start.6) | collective-permute-done | bytes 32800 | tf_op jit(solution)/shard_map/ppermute | solution.py:120
  17.9 0.6 %select_add_fusion = f32[8,1024]{1,0:T(8,128)} fusion(f32[8,1024]{1,0:T(8,128)S(1)} %collective-permute-done.6, f32[16,1024]{1,0:T(8,128)S(1)} %convert_add_fusion, pred[]{:T(512)S(6)} %eq.3), kind=kLoop, calls=%fused_computation.2 | loop fusion | flops 16384 | bytes 131073 | tf_op jit(solution)/shard_map/add | solution.py:130
  (3 shorter events, 0.0 us)
Async XLA Ops:
  0.0 9.9 %copy-start = (bf16[16,1536]{1,0:T(8,128)(2,1)S(1)}, bf16[16,1536]{1,0:T(8,128)(2,1)}, u32[]{:S(2)}) copy-start(bf16[16,1536]{1,0:T(8,128)(2,1)} %refs_0_.1) | copy-start | bytes 147460
  0.0 8.2 %collective-permute-start = (bf16[16,1536]{1,0:T(8,128)(2,1)}, bf16[16,1536]{1,0:T(8,128)(2,1)S(1)}, u32[]{:S(2)}, u32[]{:S(2)}) collective-permute-start(bf16[16,1536]{1,0:T(8,128)(2,1)} %refs_0_.1), channel_id=1, source_target_pairs={{0,2},{1,3},{2,1},{3,0},{4,6},{5,7},{6,5},{7,4},{8,10},{9,11},{10,... | collective-permute-start | bytes 147464 | tf_op jit(solution)/shard_map/ppermute | solution.py:82
  4.0 5.4 %collective-permute-start.1 = (bf16[16,1536]{1,0:T(8,128)(2,1)}, bf16[16,1536]{1,0:T(8,128)(2,1)S(1)}, u32[]{:S(2)}, u32[]{:S(2)}) collective-permute-start(bf16[16,1536]{1,0:T(8,128)(2,1)} %refs_0_.1), channel_id=1, source_target_pairs={{0,3},{1,2},{2,0},{3,1},{4,7},{5,6},{6,4},{7,5},{8,11},{9,10},{10,... | collective-permute-start | bytes 147464 | tf_op jit(solution)/shard_map/ppermute | solution.py:82
  5.1 4.8 %collective-permute-start.2 = (bf16[16,1536]{1,0:T(8,128)(2,1)}, bf16[16,1536]{1,0:T(8,128)(2,1)S(1)}, u32[]{:S(2)}, u32[]{:S(2)}) collective-permute-start(bf16[16,1536]{1,0:T(8,128)(2,1)} %refs_0_.1), channel_id=1, source_target_pairs={{0,1},{1,0},{2,3},{3,2},{4,5},{5,4},{6,7},{7,6},{8,9},{9,8},{10,11... | collective-permute-start | bytes 147464 | tf_op jit(solution)/shard_map/ppermute | solution.py:82
  10.8 1.7 %collective-permute-start.4 = (f32[16,1024]{1,0:T(8,128)S(1)}, f32[16,1024]{1,0:T(8,128)S(1)}, u32[]{:S(2)}, u32[]{:S(2)}) collective-permute-start(f32[16,1024]{1,0:T(8,128)S(1)} %get-tuple-element.18), channel_id=1, source_target_pairs={{0,4},{4,0},{1,5},{5,1},{2,6},{6,2},{3,7},{7,3},{8,12},{12,8},{9,1... | collective-permute-start | bytes 196616 | tf_op jit(solution)/shard_map/ppermute | solution.py:120
  10.9 4.0 %collective-permute-start.3 = (bf16[16,1024]{1,0:T(8,128)(2,1)S(1)}, bf16[16,1024]{1,0:T(8,128)(2,1)S(1)}, u32[]{:S(2)}, u32[]{:S(2)}) collective-permute-start(bf16[16,1024]{1,0:T(8,128)(2,1)S(1)} %get-tuple-element.16), channel_id=1, source_target_pairs={{0,16},{8,24},{16,0},{24,8},{1,17},{9,25},{17,1},{25,9},{2,18},{10... | collective-permute-start | bytes 98312 | tf_op jit(solution)/shard_map/ppermute | solution.py:124
  12.5 4.1 %collective-permute-start.5 = (bf16[16,1024]{1,0:T(8,128)(2,1)S(1)}, bf16[16,1024]{1,0:T(8,128)(2,1)S(1)}, u32[]{:S(2)}, u32[]{:S(2)}) collective-permute-start(bf16[16,1024]{1,0:T(8,128)(2,1)S(1)} %add_convert_fusion), channel_id=1, source_target_pairs={{0,8},{4,28},{8,0},{12,20},{16,24},{20,12},{24,16},{28,4},{1,9},{5... | collective-permute-start | bytes 98312 | tf_op jit(solution)/shard_map/ppermute | solution.py:126
  16.6 1.3 %collective-permute-start.6 = (f32[8,1024]{1,0:T(8,128)S(1)}, f32[8,1024]{1,0:T(8,128)S(1)}, u32[]{:S(2)}, u32[]{:S(2)}) collective-permute-start(f32[8,1024]{1,0:T(8,128)S(1)} %slice_select_fusion), channel_id=1, source_target_pairs={{0,4},{4,0},{1,5},{5,1},{2,6},{6,2},{3,7},{7,3},{8,12},{12,8},{9,1... | collective-permute-start | bytes 98312 | tf_op jit(solution)/shard_map/ppermute | solution.py:120

commit v4 on v3

--- a/solution.py
+++ b/solution.py
@@ -10,7 +10,7 @@
 SHARDS = ("section", "half")
 DIRECT = 4
 ROWS = 64
-SHUFFLES = ((2, 3, 1, 0), (3, 2, 0, 1), (1, 0, 3, 2))
+SHUFFLES = ((1, 3, 2, 0), (2, 1, 0, 3), (3, 0, 1, 2), (0, 2, 3, 1))
 NEAR = (1, 3)
 
 
@@ -31,24 +31,23 @@
     copies[2].wait()
 
 
-def local_scores(n, direct, *refs, far):
-    blocks, (train_t, precond, factor), outs = refs[:-6 - len(far)], refs[-6 - len(far):-3 - len(far)], refs[-3 - len(far):]
-    own, near, swap, aways = outs[0], outs[1], outs[2], outs[3:]
+def local_scores(n, blocks_in, *refs, far):
+    blocks, (train_t, precond, factor, own, near, swap, *aways), queries = refs[:blocks_in], refs[blocks_in:-1], refs[-1]
     mods, feat = precond.shape[0], precond.shape[1]
-    q_rows = blocks[0].shape[0] if direct else blocks[0].shape[0] // n
+    q_rows = queries.shape[0] // n
     own_rows = own.shape[0]
     unit = min(q_rows, own_rows)
     dp, section, half = (lax.axis_index(a) for a in ("dp", "section", "half"))
     routes = [(0, own), (jnp.where(half == 0, *NEAR), near), (jnp.where(half == 0, *NEAR[::-1]), swap)] + list(zip(far, aways))
 
-    def work(lhs, rows, first_row):
+    def work(lhs, rows, first):
         parts = []
         for m in range(mods):
-            pre = jnp.dot(lhs(slice(m * feat, (m + 1) * feat)), precond[m], preferred_element_type=jnp.float32)
+            pre = jnp.dot(lhs[:, m * feat:(m + 1) * feat], precond[m], preferred_element_type=jnp.float32)
             parts.append((pre * factor[m]).astype(jnp.bfloat16))
         scores = jnp.dot(jnp.concatenate(parts, axis=1), train_t[...], preferred_element_type=jnp.float32)
         for i in range(rows // unit):
-            row = first_row(i * unit)
+            row = first + i * unit
             away, at = (row // own_rows) ^ section, pl.multiple_of(lax.rem(row, own_rows), unit)
             value = scores[i * unit:(i + 1) * unit]
             for distance, out in routes:
@@ -57,16 +56,17 @@
                 def _(out=out):
                     out[pl.ds(at, unit), :] = value.astype(out.dtype)
 
-    if direct:
-        owners = [dp]
-        for shuffle in SHUFFLES:
-            owners.append(sum(jnp.where(dp == target, source, 0) for source, target in enumerate(shuffle)))
-        work(lambda c: jnp.concatenate([b[:, c] for b in blocks], axis=0), n * q_rows, lambda r: owners[r // q_rows] * q_rows + r % q_rows)
+    if blocks_in > 1:
+        for shuffle, block in zip(SHUFFLES, blocks[1:]):
+            owner = sum(jnp.where(dp == target, source, 0) for source, target in enumerate(shuffle))
+            queries[pl.ds(pl.multiple_of(owner * q_rows, q_rows), q_rows), :] = block[...]
+        queries[pl.ds(pl.multiple_of(dp * q_rows, q_rows), q_rows), :] = blocks[0][...]
+        work(queries, n * q_rows, 0)
     else:
 
         def step(c, carry):
             base = pl.multiple_of(c * ROWS, ROWS)
-            work(lambda cols: blocks[0][pl.ds(base, ROWS), cols], ROWS, lambda r: base + r)
+            work(blocks[0].at[pl.ds(base, ROWS)], ROWS, base)
             return carry
 
         lax.fori_loop(0, n * q_rows // ROWS, step, 0)
@@ -79,7 +79,10 @@
     own_rows = n * query.shape[0] // sections
     direct = n == DIRECT
     if direct:
-        blocks = [query] + [lax.ppermute(query, "dp", list(enumerate(s))) for s in SHUFFLES]
+        blocks = [query] + [
+            lax.ppermute(query, ("half", "dp"), [(n * h + i, n * (h if i != t else 1 - h) + t) for h in range(2) for i, t in enumerate(s)])
+            for s in SHUFFLES
+        ]
     else:
         blocks = [lax.all_gather(query, "dp", axis=0, tiled=True)]
 
@@ -108,10 +111,11 @@
     shape = (own_rows, cols)
     whole, half_width = jax.ShapeDtypeStruct(shape, jnp.float32), jax.ShapeDtypeStruct(shape, jnp.bfloat16)
     own, near, swap, *aways = pl.pallas_call(
-        functools.partial(local_scores, n, direct, far=far),
+        functools.partial(local_scores, n, len(blocks), far=far),
         out_shape=(whole, whole, whole) + (half_width,) * len(far),
         in_specs=[vmem] * (len(blocks) + 3),
         out_specs=(vmem,) * (3 + len(far)),
+        scratch_shapes=[pltpu.VMEM((n * query.shape[0], feats), query.dtype)],
         compiler_params=pltpu.CompilerParams(vmem_limit_bytes=48 * 2**20),
         name="local_scores",
     )(*blocks, *staged)

time: 18.7 us -> 18 us (0.963)
  waiting for transfers between devices: 5.49 us -> 5.05 us
  starting transfers between devices: 8.9 us -> 8.63 us
    ppermute x3 -> x4, waiting for transfers between devices: 1.72 us -> 1.28 us  [per_device(): lax.ppermute(query, ('half', 'dp'), [(n * h + i, n * (h if i != t else 1...]
    ppermute x3 -> x4, starting transfers between devices: 5.62 us -> 5.34 us  [per_device(): lax.ppermute(query, ('half', 'dp'), [(n * h + i, n * (h if i != t else 1...]
  transfers between devices with their start and end apart: 7 -> 8, of which waited for: 5 -> 5; matrix products, arithmetic and copies ran while one was open for 0% -> 0% of each run, Pallas kernels for 14% -> 14%
where the time goes in v4:
time: 18 us; the launch traced here: 17.8 us
  starting transfers between devices  8.63 us (48%)
  waiting for transfers between devices  5.05 us (28%)
  Pallas kernels  3.44 us (19%)
  other arithmetic  0.65 us (4%)
    ppermute x4, starting transfers between devices, per_device(): lax.ppermute(query, ('half', 'dp'), [(n * h + i, n * (h if i != t else 1...  5.34 us
    pallas_call x1, Pallas kernels, per_device(): pl.pallas_call(functools.partial(stage, pieces), out_shape=(pltpu.VMEM((f...  2.53 us
    ppermute x1, waiting for transfers between devices, per_device(): own = own + lax.ppermute(near, SHARDS, pairs).astype(jnp.float32)  1.75 us
    ppermute x1, starting transfers between devices, per_device(): lax.ppermute(away, 'section', [(i, i ^ s) for i in range(sections)])  1.59 us
    ppermute x1, starting transfers between devices, per_device(): own = own + lax.ppermute(near, SHARDS, pairs).astype(jnp.float32)  1.56 us
    ppermute x4, waiting for transfers between devices, per_device(): lax.ppermute(query, ('half', 'dp'), [(n * h + i, n * (h if i != t else 1...  1.28 us
    ppermute x2, waiting for transfers between devices, across(): return lax.ppermute(x, 'half', [(0, 1), (1, 0)])  1.2 us
    pallas_call x1, Pallas kernels, per_device(): pl.pallas_call(functools.partial(local_scores, n, len(blocks), far=far),...  0.91 us
  transfers between devices with their start and end apart: 8, of which 5 were waited for; matrix products, arithmetic and copies ran while one was open for 0% of the time, Pallas kernels for 14%

profile of v4, /device:TPU:0, one launch (start us, length us, event | category | flops | bytes accessed | tf_op | source)
XLA Modules:
  0.0 17.8 jit_solution(4441910678470095898)
XLA Ops:
  0.0 0.0 copy-start
  0.0 3.0 %collective-permute-start = (bf16[16,1536]{1,0:T(8,128)(2,1)}, bf16[16,1536]{1,0:T(8,128)(2,1)S(1)}, u32[]{:S(2)}, u32[]{:S(2)}) collective-permute-start(bf16[16,1536]{1,0:T(8,128)(2,1)} %refs_0_.1), channel_id=1, source_target_pairs={{0,1},{1,3},{2,6},{3,0},{4,5},{5,7},{6,2},{7,4},{8,9},{9,11},{10,1... | collective-permute-start | bytes 147464 | tf_op jit(solution)/shard_map/ppermute | solution.py:83
  3.0 1.1 %collective-permute-start.1 = (bf16[16,1536]{1,0:T(8,128)(2,1)}, bf16[16,1536]{1,0:T(8,128)(2,1)S(1)}, u32[]{:S(2)}, u32[]{:S(2)}) collective-permute-start(bf16[16,1536]{1,0:T(8,128)(2,1)} %refs_0_.1), channel_id=1, source_target_pairs={{0,2},{1,5},{2,0},{3,7},{4,6},{5,1},{6,4},{7,3},{8,10},{9,13},{10,... | collective-permute-start | bytes 147464 | tf_op jit(solution)/shard_map/ppermute | solution.py:83
  4.1 1.1 %collective-permute-start.2 = (bf16[16,1536]{1,0:T(8,128)(2,1)}, bf16[16,1536]{1,0:T(8,128)(2,1)S(1)}, u32[]{:S(2)}, u32[]{:S(2)}) collective-permute-start(bf16[16,1536]{1,0:T(8,128)(2,1)} %refs_0_.1), channel_id=1, source_target_pairs={{0,3},{1,0},{2,1},{3,2},{4,7},{5,4},{6,5},{7,6},{8,11},{9,8},{10,9... | collective-permute-start | bytes 147464 | tf_op jit(solution)/shard_map/ppermute | solution.py:83
  5.2 0.2 collective-permute-start.3
  5.3 2.5 %stage.1 = (bf16[1536,1024]{1,0:T(8,128)(2,1)S(1)}, bf16[6,256,256]{2,1,0:T(8,128)(2,1)S(1)}, f32[6,1,256]{2,1,0:T(1,128)S(1)}) custom-call(bf16[1024,1536]{1,0:T(8,128)(2,1)} %train.1, bf16[6,256,256]{2,1,0:T(8,128)(2,1)} %precond.1, s32[6]{0:T(128)} %kind.1, f32[7]{0:T(128)} %scale.1), custom_call_target="tpu_custom_call" | custom-call | bytes 6291456 | tf_op jit(solution)/shard_map/stage/pallas_call | solution.py:91
  7.9 0.0 collective-permute-done.refs_1_
  7.9 0.4 %collective-permute-done.1.refs_2_ = bf16[16,1536]{1,0:T(8,128)(2,1)S(1)} collective-permute-done((bf16[16,1536]{1,0:T(8,128)(2,1)}, bf16[16,1536]{1,0:T(8,128)(2,1)S(1)}, u32[]{:S(2)}, u32[]{:S(2)}) %collective-permute-start.1) | collective-permute-done | bytes 49184 | tf_op jit(solution)/shard_map/ppermute | solution.py:83
  8.3 0.9 %collective-permute-done.2.refs_3_ = bf16[16,1536]{1,0:T(8,128)(2,1)S(1)} collective-permute-done((bf16[16,1536]{1,0:T(8,128)(2,1)}, bf16[16,1536]{1,0:T(8,128)(2,1)S(1)}, u32[]{:S(2)}, u32[]{:S(2)}) %collective-permute-start.2) | collective-permute-done | bytes 49184 | tf_op jit(solution)/shard_map/ppermute | solution.py:83
  9.2 0.0 collective-permute-done.3.refs_4_
  9.2 0.0 copy-done
  9.2 0.9 %local_scores.1 = (f32[16,1024]{1,0:T(8,128)S(1)}, f32[16,1024]{1,0:T(8,128)S(1)}, f32[16,1024]{1,0:T(8,128)S(1)}, bf16[16,1024]{1,0:T(8,128)(2,1)S(1)}) custom-call(bf16[16,1536]{1,0:T(8,128)(2,1)S(1)} %copy-done, bf16[16,1536]{1,0:T(8,128)(2,1)S(1)} %collective-permute-done.refs_1_, bf16[16,1536]{1,0:T(8,128)(2,1)S(1)} %collective-permute-done.1.refs_2_, ...), custom_call_target="tpu_custom_call" | custom-call | tf_op jit(solution)/shard_map/local_scores/pallas_call | solution.py:113
  10.1 0.1 collective-permute-start.5
  10.2 1.6 %collective-permute-start.4 = (bf16[16,1024]{1,0:T(8,128)(2,1)S(1)}, bf16[16,1024]{1,0:T(8,128)(2,1)S(1)}, u32[]{:S(2)}, u32[]{:S(2)}) collective-permute-start(bf16[16,1024]{1,0:T(8,128)(2,1)S(1)} %get-tuple-element.16), channel_id=1, source_target_pairs={{0,16},{8,24},{16,0},{24,8},{1,17},{9,25},{17,1},{25,9},{2,18},{10... | collective-permute-start | bytes 98312 | tf_op jit(solution)/shard_map/ppermute | solution.py:128
  11.8 0.0 collective-permute-done.5
  11.8 1.6 %collective-permute-start.6 = (bf16[16,1024]{1,0:T(8,128)(2,1)S(1)}, bf16[16,1024]{1,0:T(8,128)(2,1)S(1)}, u32[]{:S(2)}, u32[]{:S(2)}) collective-permute-start(bf16[16,1024]{1,0:T(8,128)(2,1)S(1)} %add_convert_fusion), channel_id=1, source_target_pairs={{0,8},{4,28},{8,0},{12,20},{16,24},{20,12},{24,16},{28,4},{1,9},{5... | collective-permute-start | bytes 98312 | tf_op jit(solution)/shard_map/ppermute | solution.py:130
  13.3 0.8 %collective-permute-done.4 = bf16[16,1024]{1,0:T(8,128)(2,1)S(1)} collective-permute-done((bf16[16,1024]{1,0:T(8,128)(2,1)S(1)}, bf16[16,1024]{1,0:T(8,128)(2,1)S(1)}, u32[]{:S(2)}, u32[]{:S(2)}) %collective-permute-start.4) | collective-permute-done | bytes 32800 | tf_op jit(solution)/shard_map/ppermute | solution.py:128
  14.2 1.8 %collective-permute-done.6 = bf16[16,1024]{1,0:T(8,128)(2,1)S(1)} collective-permute-done((bf16[16,1024]{1,0:T(8,128)(2,1)S(1)}, bf16[16,1024]{1,0:T(8,128)(2,1)S(1)}, u32[]{:S(2)}, u32[]{:S(2)}) %collective-permute-start.6) | collective-permute-done | bytes 32800 | tf_op jit(solution)/shard_map/ppermute | solution.py:130
  15.9 0.1 collective-permute-start.7
  16.0 1.2 %collective-permute-done.7 = f32[8,1024]{1,0:T(8,128)S(1)} collective-permute-done((f32[8,1024]{1,0:T(8,128)S(1)}, f32[8,1024]{1,0:T(8,128)S(1)}, u32[]{:S(2)}, u32[]{:S(2)}) %collective-permute-start.7) | collective-permute-done | bytes 32800 | tf_op jit(solution)/shard_map/ppermute | solution.py:124
  17.2 0.6 %select_add_fusion = f32[8,1024]{1,0:T(8,128)} fusion(f32[8,1024]{1,0:T(8,128)S(1)} %collective-permute-done.7, f32[16,1024]{1,0:T(8,128)S(1)} %convert_add_fusion, pred[]{:T(512)S(6)} %eq.3), kind=kLoop, calls=%fused_computation.2 | loop fusion | flops 16384 | bytes 131073 | tf_op jit(solution)/shard_map/add | solution.py:134
  (3 shorter events, 0.0 us)
Async XLA Ops:
  0.0 9.2 %copy-start = (bf16[16,1536]{1,0:T(8,128)(2,1)S(1)}, bf16[16,1536]{1,0:T(8,128)(2,1)}, u32[]{:S(2)}) copy-start(bf16[16,1536]{1,0:T(8,128)(2,1)} %refs_0_.1) | copy-start | bytes 147460
  0.0 7.9 %collective-permute-start = (bf16[16,1536]{1,0:T(8,128)(2,1)}, bf16[16,1536]{1,0:T(8,128)(2,1)S(1)}, u32[]{:S(2)}, u32[]{:S(2)}) collective-permute-start(bf16[16,1536]{1,0:T(8,128)(2,1)} %refs_0_.1), channel_id=1, source_target_pairs={{0,1},{1,3},{2,6},{3,0},{4,5},{5,7},{6,2},{7,4},{8,9},{9,11},{10,1... | collective-permute-start | bytes 147464 | tf_op jit(solution)/shard_map/ppermute | solution.py:83
  3.0 5.3 %collective-permute-start.1 = (bf16[16,1536]{1,0:T(8,128)(2,1)}, bf16[16,1536]{1,0:T(8,128)(2,1)S(1)}, u32[]{:S(2)}, u32[]{:S(2)}) collective-permute-start(bf16[16,1536]{1,0:T(8,128)(2,1)} %refs_0_.1), channel_id=1, source_target_pairs={{0,2},{1,5},{2,0},{3,7},{4,6},{5,1},{6,4},{7,3},{8,10},{9,13},{10,... | collective-permute-start | bytes 147464 | tf_op jit(solution)/shard_map/ppermute | solution.py:83
  4.1 5.1 %collective-permute-start.2 = (bf16[16,1536]{1,0:T(8,128)(2,1)}, bf16[16,1536]{1,0:T(8,128)(2,1)S(1)}, u32[]{:S(2)}, u32[]{:S(2)}) collective-permute-start(bf16[16,1536]{1,0:T(8,128)(2,1)} %refs_0_.1), channel_id=1, source_target_pairs={{0,3},{1,0},{2,1},{3,2},{4,7},{5,4},{6,5},{7,6},{8,11},{9,8},{10,9... | collective-permute-start | bytes 147464 | tf_op jit(solution)/shard_map/ppermute | solution.py:83
  5.2 4.0 %collective-permute-start.3 = (bf16[16,1536]{1,0:T(8,128)(2,1)}, bf16[16,1536]{1,0:T(8,128)(2,1)S(1)}, u32[]{:S(2)}, u32[]{:S(2)}) collective-permute-start(bf16[16,1536]{1,0:T(8,128)(2,1)} %refs_0_.1), channel_id=1, source_target_pairs={{0,4},{1,2},{2,3},{3,1},{4,0},{5,6},{6,7},{7,5},{8,12},{9,10},{10,... | collective-permute-start | bytes 147464 | tf_op jit(solution)/shard_map/ppermute | solution.py:83
  10.1 1.7 %collective-permute-start.5 = (f32[16,1024]{1,0:T(8,128)S(1)}, f32[16,1024]{1,0:T(8,128)S(1)}, u32[]{:S(2)}, u32[]{:S(2)}) collective-permute-start(f32[16,1024]{1,0:T(8,128)S(1)} %get-tuple-element.18), channel_id=1, source_target_pairs={{0,4},{4,0},{1,5},{5,1},{2,6},{6,2},{3,7},{7,3},{8,12},{12,8},{9,1... | collective-permute-start | bytes 196616 | tf_op jit(solution)/shard_map/ppermute | solution.py:124
  10.2 4.0 %collective-permute-start.4 = (bf16[16,1024]{1,0:T(8,128)(2,1)S(1)}, bf16[16,1024]{1,0:T(8,128)(2,1)S(1)}, u32[]{:S(2)}, u32[]{:S(2)}) collective-permute-start(bf16[16,1024]{1,0:T(8,128)(2,1)S(1)} %get-tuple-element.16), channel_id=1, source_target_pairs={{0,16},{8,24},{16,0},{24,8},{1,17},{9,25},{17,1},{25,9},{2,18},{10... | collective-permute-start | bytes 98312 | tf_op jit(solution)/shard_map/ppermute | solution.py:128
  11.8 4.1 %collective-permute-start.6 = (bf16[16,1024]{1,0:T(8,128)(2,1)S(1)}, bf16[16,1024]{1,0:T(8,128)(2,1)S(1)}, u32[]{:S(2)}, u32[]{:S(2)}) collective-permute-start(bf16[16,1024]{1,0:T(8,128)(2,1)S(1)} %add_convert_fusion), channel_id=1, source_target_pairs={{0,8},{4,28},{8,0},{12,20},{16,24},{20,12},{24,16},{28,4},{1,9},{5... | collective-permute-start | bytes 98312 | tf_op jit(solution)/shard_map/ppermute | solution.py:130
  15.9 1.3 %collective-permute-start.7 = (f32[8,1024]{1,0:T(8,128)S(1)}, f32[8,1024]{1,0:T(8,128)S(1)}, u32[]{:S(2)}, u32[]{:S(2)}) collective-permute-start(f32[8,1024]{1,0:T(8,128)S(1)} %slice_select_fusion), channel_id=1, source_target_pairs={{0,4},{4,0},{1,5},{5,1},{2,6},{6,2},{3,7},{7,3},{8,12},{12,8},{9,1... | collective-permute-start | bytes 98312 | tf_op jit(solution)/shard_map/ppermute | solution.py:124

commit v5 on v4

--- a/solution.py
+++ b/solution.py
@@ -31,42 +31,51 @@
     copies[2].wait()
 
 
-def local_scores(n, blocks_in, *refs, far):
-    blocks, (train_t, precond, factor, own, near, swap, *aways), queries = refs[:blocks_in], refs[blocks_in:-1], refs[-1]
+def weighted_scores(lhs, train_t, precond, factor):
     mods, feat = precond.shape[0], precond.shape[1]
+    parts = []
+    for m in range(mods):
+        pre = jnp.dot(lhs[:, m * feat:(m + 1) * feat], precond[m], preferred_element_type=jnp.float32)
+        parts.append((pre * factor[m]).astype(jnp.bfloat16))
+    return jnp.dot(jnp.concatenate(parts, axis=1), train_t[...], preferred_element_type=jnp.float32)
+
+
+def local_scores(n, blocks_in, far, *refs):
+    blocks, (train_t, precond, factor, *outs), queries = refs[:blocks_in], refs[blocks_in:-1], refs[-1]
     q_rows = queries.shape[0] // n
-    own_rows = own.shape[0]
-    unit = min(q_rows, own_rows)
+    own_rows = outs[0].shape[0]
     dp, section, half = (lax.axis_index(a) for a in ("dp", "section", "half"))
-    routes = [(0, own), (jnp.where(half == 0, *NEAR), near), (jnp.where(half == 0, *NEAR[::-1]), swap)] + list(zip(far, aways))
-
-    def work(lhs, rows, first):
-        parts = []
-        for m in range(mods):
-            pre = jnp.dot(lhs[:, m * feat:(m + 1) * feat], precond[m], preferred_element_type=jnp.float32)
-            parts.append((pre * factor[m]).astype(jnp.bfloat16))
-        scores = jnp.dot(jnp.concatenate(parts, axis=1), train_t[...], preferred_element_type=jnp.float32)
-        for i in range(rows // unit):
-            row = first + i * unit
-            away, at = (row // own_rows) ^ section, pl.multiple_of(lax.rem(row, own_rows), unit)
-            value = scores[i * unit:(i + 1) * unit]
-            for distance, out in routes:
-
-                @pl.when(away == distance)
-                def _(out=out):
-                    out[pl.ds(at, unit), :] = value.astype(out.dtype)
+    served = jnp.where(half == 0, *NEAR)
+    distances = (0, served, sum(NEAR) - served) + far
 
     if blocks_in > 1:
+
+        def put(owner, block):
+            away = owner ^ section
+            place = sum(jnp.where(away == distance, i, 0) for i, distance in enumerate(distances))
+            queries[pl.ds(pl.multiple_of(place * q_rows, q_rows), q_rows), :] = block[...]
+
         for shuffle, block in zip(SHUFFLES, blocks[1:]):
-            owner = sum(jnp.where(dp == target, source, 0) for source, target in enumerate(shuffle))
-            queries[pl.ds(pl.multiple_of(owner * q_rows, q_rows), q_rows), :] = block[...]
-        queries[pl.ds(pl.multiple_of(dp * q_rows, q_rows), q_rows), :] = blocks[0][...]
-        work(queries, n * q_rows, 0)
+            put(sum(jnp.where(dp == target, source, 0) for source, target in enumerate(shuffle)), block)
+        put(dp, blocks[0])
+        scores = weighted_scores(queries, train_t, precond, factor)
+        for i, out in enumerate(outs):
+            out[...] = scores[i * own_rows:(i + 1) * own_rows].astype(out.dtype)
     else:
+        unit = min(q_rows, own_rows)
 
         def step(c, carry):
             base = pl.multiple_of(c * ROWS, ROWS)
-            work(blocks[0].at[pl.ds(base, ROWS)], ROWS, base)
+            scores = weighted_scores(blocks[0].at[pl.ds(base, ROWS)], train_t, precond, factor)
+            for i in range(ROWS // unit):
+                row = base + i * unit
+                away, at = (row // own_rows) ^ section, pl.multiple_of(lax.rem(row, own_rows), unit)
+                for distance, out in zip(distances, outs):
+
+                    @pl.when(away == distance)
+                    def _(i=i, at=at, out=out):
+                        out[pl.ds(at, unit), :] = scores[i * unit:(i + 1) * unit].astype(out.dtype)
+
             return carry
 
         lax.fori_loop(0, n * q_rows // ROWS, step, 0)
@@ -77,7 +86,7 @@
     mods, feat = precond.shape[:2]
     cols, feats = train.shape
     own_rows = n * query.shape[0] // sections
-    direct = n == DIRECT
+    direct = n == sections == DIRECT
     if direct:
         blocks = [query] + [
             lax.ppermute(query, ("half", "dp"), [(n * h + i, n * (h if i != t else 1 - h) + t) for h in range(2) for i, t in enumerate(s)])
@@ -111,7 +120,7 @@
     shape = (own_rows, cols)
     whole, half_width = jax.ShapeDtypeStruct(shape, jnp.float32), jax.ShapeDtypeStruct(shape, jnp.bfloat16)
     own, near, swap, *aways = pl.pallas_call(
-        functools.partial(local_scores, n, len(blocks), far=far),
+        functools.partial(local_scores, n, len(blocks), far),
         out_shape=(whole, whole, whole) + (half_width,) * len(far),
         in_specs=[vmem] * (len(blocks) + 3),
         out_specs=(vmem,) * (3 + len(far)),

time: 18 us -> 17.9 us (level)
  no operation moved by 1% of the time
where the time goes in v5:
time: 17.9 us; the launch traced here: 17.8 us
  starting transfers between devices  8.62 us (48%)
  waiting for transfers between devices  5.05 us (28%)
  Pallas kernels  3.37 us (19%)
  other arithmetic  0.65 us (4%)
    ppermute x4, starting transfers between devices, per_device(): lax.ppermute(query, ('half', 'dp'), [(n * h + i, n * (h if i != t else 1...  5.34 us
    pallas_call x1, Pallas kernels, per_device(): pl.pallas_call(functools.partial(stage, pieces), out_shape=(pltpu.VMEM((f...  2.53 us
    ppermute x1, waiting for transfers between devices, per_device(): own = own + lax.ppermute(near, SHARDS, pairs).astype(jnp.float32)  1.75 us
    ppermute x1, starting transfers between devices, per_device(): lax.ppermute(away, 'section', [(i, i ^ s) for i in range(sections)])  1.58 us
    ppermute x1, starting transfers between devices, per_device(): own = own + lax.ppermute(near, SHARDS, pairs).astype(jnp.float32)  1.56 us
    ppermute x4, waiting for transfers between devices, per_device(): lax.ppermute(query, ('half', 'dp'), [(n * h + i, n * (h if i != t else 1...  1.28 us
    ppermute x2, waiting for transfers between devices, across(): return lax.ppermute(x, 'half', [(0, 1), (1, 0)])  1.2 us
    pallas_call x1, Pallas kernels, per_device(): pl.pallas_call(functools.partial(local_scores, n, len(blocks), far), out_...  0.84 us
  transfers between devices with their start and end apart: 8, of which 5 were waited for; matrix products, arithmetic and copies ran while one was open for 0% of the time, Pallas kernels for 14%

profile of v5, /device:TPU:0, one launch (start us, length us, event | category | flops | bytes accessed | tf_op | source)
XLA Modules:
  0.0 17.8 jit_solution(13396099112129731418)
XLA Ops:
  0.0 0.0 copy-start
  0.0 3.0 %collective-permute-start = (bf16[16,1536]{1,0:T(8,128)(2,1)}, bf16[16,1536]{1,0:T(8,128)(2,1)S(1)}, u32[]{:S(2)}, u32[]{:S(2)}) collective-permute-start(bf16[16,1536]{1,0:T(8,128)(2,1)} %refs_0_.1), channel_id=1, source_target_pairs={{0,1},{1,3},{2,6},{3,0},{4,5},{5,7},{6,2},{7,4},{8,9},{9,11},{10,1... | collective-permute-start | bytes 147464 | tf_op jit(solution)/shard_map/ppermute | solution.py:92
  3.0 1.1 %collective-permute-start.1 = (bf16[16,1536]{1,0:T(8,128)(2,1)}, bf16[16,1536]{1,0:T(8,128)(2,1)S(1)}, u32[]{:S(2)}, u32[]{:S(2)}) collective-permute-start(bf16[16,1536]{1,0:T(8,128)(2,1)} %refs_0_.1), channel_id=1, source_target_pairs={{0,2},{1,5},{2,0},{3,7},{4,6},{5,1},{6,4},{7,3},{8,10},{9,13},{10,... | collective-permute-start | bytes 147464 | tf_op jit(solution)/shard_map/ppermute | solution.py:92
  4.1 1.1 %collective-permute-start.2 = (bf16[16,1536]{1,0:T(8,128)(2,1)}, bf16[16,1536]{1,0:T(8,128)(2,1)S(1)}, u32[]{:S(2)}, u32[]{:S(2)}) collective-permute-start(bf16[16,1536]{1,0:T(8,128)(2,1)} %refs_0_.1), channel_id=1, source_target_pairs={{0,3},{1,0},{2,1},{3,2},{4,7},{5,4},{6,5},{7,6},{8,11},{9,8},{10,9... | collective-permute-start | bytes 147464 | tf_op jit(solution)/shard_map/ppermute | solution.py:92
  5.2 0.2 collective-permute-start.3
  5.3 2.5 %stage.1 = (bf16[1536,1024]{1,0:T(8,128)(2,1)S(1)}, bf16[6,256,256]{2,1,0:T(8,128)(2,1)S(1)}, f32[6,1,256]{2,1,0:T(1,128)S(1)}) custom-call(bf16[1024,1536]{1,0:T(8,128)(2,1)} %train.1, bf16[6,256,256]{2,1,0:T(8,128)(2,1)} %precond.1, s32[6]{0:T(128)} %kind.1, f32[7]{0:T(128)} %scale.1), custom_call_target="tpu_custom_call" | custom-call | bytes 6291456 | tf_op jit(solution)/shard_map/stage/pallas_call | solution.py:100
  7.9 0.0 collective-permute-done.refs_1_
  7.9 0.4 %collective-permute-done.1.refs_2_ = bf16[16,1536]{1,0:T(8,128)(2,1)S(1)} collective-permute-done((bf16[16,1536]{1,0:T(8,128)(2,1)}, bf16[16,1536]{1,0:T(8,128)(2,1)S(1)}, u32[]{:S(2)}, u32[]{:S(2)}) %collective-permute-start.1) | collective-permute-done | bytes 49184 | tf_op jit(solution)/shard_map/ppermute | solution.py:92
  8.3 0.9 %collective-permute-done.2.refs_3_ = bf16[16,1536]{1,0:T(8,128)(2,1)S(1)} collective-permute-done((bf16[16,1536]{1,0:T(8,128)(2,1)}, bf16[16,1536]{1,0:T(8,128)(2,1)S(1)}, u32[]{:S(2)}, u32[]{:S(2)}) %collective-permute-start.2) | collective-permute-done | bytes 49184 | tf_op jit(solution)/shard_map/ppermute | solution.py:92
  9.2 0.0 collective-permute-done.3.refs_4_
  9.2 0.0 copy-done
  9.2 0.8 %local_scores.1 = (f32[16,1024]{1,0:T(8,128)S(1)}, f32[16,1024]{1,0:T(8,128)S(1)}, f32[16,1024]{1,0:T(8,128)S(1)}, bf16[16,1024]{1,0:T(8,128)(2,1)S(1)}) custom-call(bf16[16,1536]{1,0:T(8,128)(2,1)S(1)} %copy-done, bf16[16,1536]{1,0:T(8,128)(2,1)S(1)} %collective-permute-done.refs_1_, bf16[16,1536]{1,0:T(8,128)(2,1)S(1)} %collective-permute-done.1.refs_2_, ...), custom_call_target="tpu_custom_call" | custom-call | tf_op jit(solution)/shard_map/local_scores/pallas_call | solution.py:122
  10.0 0.1 collective-permute-start.5
  10.1 1.6 %collective-permute-start.4 = (bf16[16,1024]{1,0:T(8,128)(2,1)S(1)}, bf16[16,1024]{1,0:T(8,128)(2,1)S(1)}, u32[]{:S(2)}, u32[]{:S(2)}) collective-permute-start(bf16[16,1024]{1,0:T(8,128)(2,1)S(1)} %get-tuple-element.16), channel_id=1, source_target_pairs={{0,16},{8,24},{16,0},{24,8},{1,17},{9,25},{17,1},{25,9},{2,18},{10... | collective-permute-start | bytes 98312 | tf_op jit(solution)/shard_map/ppermute | solution.py:137
  11.7 0.0 collective-permute-done.5
  11.7 1.6 %collective-permute-start.6 = (bf16[16,1024]{1,0:T(8,128)(2,1)S(1)}, bf16[16,1024]{1,0:T(8,128)(2,1)S(1)}, u32[]{:S(2)}, u32[]{:S(2)}) collective-permute-start(bf16[16,1024]{1,0:T(8,128)(2,1)S(1)} %add_convert_fusion), channel_id=1, source_target_pairs={{0,8},{4,28},{8,0},{12,20},{16,24},{20,12},{24,16},{28,4},{1,9},{5... | collective-permute-start | bytes 98312 | tf_op jit(solution)/shard_map/ppermute | solution.py:139
  13.3 0.8 %collective-permute-done.4 = bf16[16,1024]{1,0:T(8,128)(2,1)S(1)} collective-permute-done((bf16[16,1024]{1,0:T(8,128)(2,1)S(1)}, bf16[16,1024]{1,0:T(8,128)(2,1)S(1)}, u32[]{:S(2)}, u32[]{:S(2)}) %collective-permute-start.4) | collective-permute-done | bytes 32800 | tf_op jit(solution)/shard_map/ppermute | solution.py:137
  14.1 1.7 %collective-permute-done.6 = bf16[16,1024]{1,0:T(8,128)(2,1)S(1)} collective-permute-done((bf16[16,1024]{1,0:T(8,128)(2,1)S(1)}, bf16[16,1024]{1,0:T(8,128)(2,1)S(1)}, u32[]{:S(2)}, u32[]{:S(2)}) %collective-permute-start.6) | collective-permute-done | bytes 32800 | tf_op jit(solution)/shard_map/ppermute | solution.py:139
  15.9 0.1 collective-permute-start.7
  15.9 1.2 %collective-permute-done.7 = f32[8,1024]{1,0:T(8,128)S(1)} collective-permute-done((f32[8,1024]{1,0:T(8,128)S(1)}, f32[8,1024]{1,0:T(8,128)S(1)}, u32[]{:S(2)}, u32[]{:S(2)}) %collective-permute-start.7) | collective-permute-done | bytes 32800 | tf_op jit(solution)/shard_map/ppermute | solution.py:133
  17.1 0.6 %select_add_fusion = f32[8,1024]{1,0:T(8,128)} fusion(f32[8,1024]{1,0:T(8,128)S(1)} %collective-permute-done.7, f32[16,1024]{1,0:T(8,128)S(1)} %convert_add_fusion, pred[]{:T(512)S(6)} %eq.3), kind=kLoop, calls=%fused_computation.2 | loop fusion | flops 16384 | bytes 131073 | tf_op jit(solution)/shard_map/add | solution.py:143
  (3 shorter events, 0.0 us)
Async XLA Ops:
  0.0 9.2 %copy-start = (bf16[16,1536]{1,0:T(8,128)(2,1)S(1)}, bf16[16,1536]{1,0:T(8,128)(2,1)}, u32[]{:S(2)}) copy-start(bf16[16,1536]{1,0:T(8,128)(2,1)} %refs_0_.1) | copy-start | bytes 147460
  0.0 7.9 %collective-permute-start = (bf16[16,1536]{1,0:T(8,128)(2,1)}, bf16[16,1536]{1,0:T(8,128)(2,1)S(1)}, u32[]{:S(2)}, u32[]{:S(2)}) collective-permute-start(bf16[16,1536]{1,0:T(8,128)(2,1)} %refs_0_.1), channel_id=1, source_target_pairs={{0,1},{1,3},{2,6},{3,0},{4,5},{5,7},{6,2},{7,4},{8,9},{9,11},{10,1... | collective-permute-start | bytes 147464 | tf_op jit(solution)/shard_map/ppermute | solution.py:92
  3.0 5.3 %collective-permute-start.1 = (bf16[16,1536]{1,0:T(8,128)(2,1)}, bf16[16,1536]{1,0:T(8,128)(2,1)S(1)}, u32[]{:S(2)}, u32[]{:S(2)}) collective-permute-start(bf16[16,1536]{1,0:T(8,128)(2,1)} %refs_0_.1), channel_id=1, source_target_pairs={{0,2},{1,5},{2,0},{3,7},{4,6},{5,1},{6,4},{7,3},{8,10},{9,13},{10,... | collective-permute-start | bytes 147464 | tf_op jit(solution)/shard_map/ppermute | solution.py:92
  4.1 5.1 %collective-permute-start.2 = (bf16[16,1536]{1,0:T(8,128)(2,1)}, bf16[16,1536]{1,0:T(8,128)(2,1)S(1)}, u32[]{:S(2)}, u32[]{:S(2)}) collective-permute-start(bf16[16,1536]{1,0:T(8,128)(2,1)} %refs_0_.1), channel_id=1, source_target_pairs={{0,3},{1,0},{2,1},{3,2},{4,7},{5,4},{6,5},{7,6},{8,11},{9,8},{10,9... | collective-permute-start | bytes 147464 | tf_op jit(solution)/shard_map/ppermute | solution.py:92
  5.2 4.0 %collective-permute-start.3 = (bf16[16,1536]{1,0:T(8,128)(2,1)}, bf16[16,1536]{1,0:T(8,128)(2,1)S(1)}, u32[]{:S(2)}, u32[]{:S(2)}) collective-permute-start(bf16[16,1536]{1,0:T(8,128)(2,1)} %refs_0_.1), channel_id=1, source_target_pairs={{0,4},{1,2},{2,3},{3,1},{4,0},{5,6},{6,7},{7,5},{8,12},{9,10},{10,... | collective-permute-start | bytes 147464 | tf_op jit(solution)/shard_map/ppermute | solution.py:92
  10.0 1.7 %collective-permute-start.5 = (f32[16,1024]{1,0:T(8,128)S(1)}, f32[16,1024]{1,0:T(8,128)S(1)}, u32[]{:S(2)}, u32[]{:S(2)}) collective-permute-start(f32[16,1024]{1,0:T(8,128)S(1)} %get-tuple-element.18), channel_id=1, source_target_pairs={{0,4},{4,0},{1,5},{5,1},{2,6},{6,2},{3,7},{7,3},{8,12},{12,8},{9,1... | collective-permute-start | bytes 196616 | tf_op jit(solution)/shard_map/ppermute | solution.py:133
  10.1 4.0 %collective-permute-start.4 = (bf16[16,1024]{1,0:T(8,128)(2,1)S(1)}, bf16[16,1024]{1,0:T(8,128)(2,1)S(1)}, u32[]{:S(2)}, u32[]{:S(2)}) collective-permute-start(bf16[16,1024]{1,0:T(8,128)(2,1)S(1)} %get-tuple-element.16), channel_id=1, source_target_pairs={{0,16},{8,24},{16,0},{24,8},{1,17},{9,25},{17,1},{25,9},{2,18},{10... | collective-permute-start | bytes 98312 | tf_op jit(solution)/shard_map/ppermute | solution.py:137
  11.7 4.1 %collective-permute-start.6 = (bf16[16,1024]{1,0:T(8,128)(2,1)S(1)}, bf16[16,1024]{1,0:T(8,128)(2,1)S(1)}, u32[]{:S(2)}, u32[]{:S(2)}) collective-permute-start(bf16[16,1024]{1,0:T(8,128)(2,1)S(1)} %add_convert_fusion), channel_id=1, source_target_pairs={{0,8},{4,28},{8,0},{12,20},{16,24},{20,12},{24,16},{28,4},{1,9},{5... | collective-permute-start | bytes 98312 | tf_op jit(solution)/shard_map/ppermute | solution.py:139
  15.9 1.3 %collective-permute-start.7 = (f32[8,1024]{1,0:T(8,128)S(1)}, f32[8,1024]{1,0:T(8,128)S(1)}, u32[]{:S(2)}, u32[]{:S(2)}) collective-permute-start(f32[8,1024]{1,0:T(8,128)S(1)} %slice_select_fusion), channel_id=1, source_target_pairs={{0,4},{4,0},{1,5},{5,1},{2,6},{6,2},{3,7},{7,3},{8,12},{12,8},{9,1... | collective-permute-start | bytes 98312 | tf_op jit(solution)/shard_map/ppermute | solution.py:133

commit v6 on v5

--- a/solution.py
+++ b/solution.py
@@ -11,7 +11,7 @@
 DIRECT = 4
 ROWS = 64
 SHUFFLES = ((1, 3, 2, 0), (2, 1, 0, 3), (3, 0, 1, 2), (0, 2, 3, 1))
-NEAR = (1, 3)
+ROUTES = ((2, 3, 0, 1), (3, 0, 1, 2), (1, 2, 3, 0))
 
 
 def stage(pieces, train, precond, kind, scale, train_t, precond_v, factor, raw, kind_s, scale_s, sems):
@@ -40,19 +40,18 @@
     return jnp.dot(jnp.concatenate(parts, axis=1), train_t[...], preferred_element_type=jnp.float32)
 
 
-def local_scores(n, blocks_in, far, *refs):
+def local_scores(n, blocks_in, routes, *refs):
     blocks, (train_t, precond, factor, *outs), queries = refs[:blocks_in], refs[blocks_in:-1], refs[-1]
     q_rows = queries.shape[0] // n
     own_rows = outs[0].shape[0]
     dp, section, half = (lax.axis_index(a) for a in ("dp", "section", "half"))
-    served = jnp.where(half == 0, *NEAR)
-    distances = (0, served, sum(NEAR) - served) + far
+    to = [sum(jnp.where(section == source, target, 0) for source, target in enumerate(route)) for route in routes]
+    homes = (section, jnp.where(half == 0, to[0], to[1]), jnp.where(half == 0, to[1], to[0]), *to[2:])
 
     if blocks_in > 1:
 
         def put(owner, block):
-            away = owner ^ section
-            place = sum(jnp.where(away == distance, i, 0) for i, distance in enumerate(distances))
+            place = sum(jnp.where(owner == home, i, 0) for i, home in enumerate(homes))
             queries[pl.ds(pl.multiple_of(place * q_rows, q_rows), q_rows), :] = block[...]
 
         for shuffle, block in zip(SHUFFLES, blocks[1:]):
@@ -69,10 +68,10 @@
             scores = weighted_scores(blocks[0].at[pl.ds(base, ROWS)], train_t, precond, factor)
             for i in range(ROWS // unit):
                 row = base + i * unit
-                away, at = (row // own_rows) ^ section, pl.multiple_of(lax.rem(row, own_rows), unit)
-                for distance, out in zip(distances, outs):
+                at = pl.multiple_of(lax.rem(row, own_rows), unit)
+                for home, out in zip(homes, outs):
 
-                    @pl.when(away == distance)
+                    @pl.when(row // own_rows == home)
                     def _(i=i, at=at, out=out):
                         out[pl.ds(at, unit), :] = scores[i * unit:(i + 1) * unit].astype(out.dtype)
 
@@ -116,11 +115,12 @@
         compiler_params=pltpu.CompilerParams(vmem_limit_bytes=32 * 2**20),
         name="stage",
     )(*(pltpu.with_memory_space_constraint(a, pltpu.HBM) for a in (train, precond, module_kind, kind_scale)))
-    far = tuple(s for s in range(1, sections) if s not in NEAR)
+    routes = ROUTES if sections == 4 else tuple(tuple(i ^ s for i in range(sections)) for s in range(1, sections))
+    far = routes[2:]
     shape = (own_rows, cols)
     whole, half_width = jax.ShapeDtypeStruct(shape, jnp.float32), jax.ShapeDtypeStruct(shape, jnp.bfloat16)
     own, near, swap, *aways = pl.pallas_call(
-        functools.partial(local_scores, n, len(blocks), far),
+        functools.partial(local_scores, n, len(blocks), routes),
         out_shape=(whole, whole, whole) + (half_width,) * len(far),
         in_specs=[vmem] * (len(blocks) + 3),
         out_specs=(vmem,) * (3 + len(far)),
@@ -133,9 +133,9 @@
         return lax.ppermute(x, "half", [(0, 1), (1, 0)])
 
     near = (near + across(swap)).astype(jnp.bfloat16)
-    for s, away in zip(far, aways):
-        own = own + lax.ppermute(away, "section", [(i, i ^ s) for i in range(sections)]).astype(jnp.float32)
-    pairs = [(2 * i + h, 2 * (i ^ NEAR[h]) + h) for i in range(sections) for h in range(2)]
+    for route, away in zip(far, aways):
+        own = own + lax.ppermute(away, "section", list(enumerate(route))).astype(jnp.float32)
+    pairs = [(2 * i + h, 2 * routes[h][i] + 1 - h) for i in range(sections) for h in range(2)]
     own = own + lax.ppermute(near, SHARDS, pairs).astype(jnp.float32)
     rows = own_rows // 2
     first = lax.axis_index("half") == 0

time: 17.9 us -> 17.5 us (0.978)
  waiting for transfers between devices: 5.05 us -> 4.75 us
    ppermute x1, waiting for transfers between devices: 1.75 us -> 0.41 us  [per_device(): own = own + lax.ppermute(near, SHARDS, pairs).astype(jnp.float32)]
    ppermute x1, waiting for transfers between devices: 0.82 us -> 1.97 us  [per_device(): lax.ppermute(away, 'section', list(enumerate(route))).astype(jnp.float32)]
    ppermute x1, starting transfers between devices: 1.56 us -> 1.34 us  [per_device(): own = own + lax.ppermute(near, SHARDS, pairs).astype(jnp.float32)]
  transfers between devices with their start and end apart: 8 -> 8, of which waited for: 5 -> 5; matrix products, arithmetic and copies ran while one was open for 0% -> 0% of each run, Pallas kernels for 14% -> 15%
where the time goes in v6:
time: 17.5 us; the launch traced here: 17.3 us
  starting transfers between devices  8.48 us (48%)
  waiting for transfers between devices  4.75 us (27%)
  Pallas kernels  3.37 us (19%)
  other arithmetic  0.65 us (4%)
    ppermute x4, starting transfers between devices, per_device(): lax.ppermute(query, ('half', 'dp'), [(n * h + i, n * (h if i != t else 1...  5.34 us
    pallas_call x1, Pallas kernels, per_device(): pl.pallas_call(functools.partial(stage, pieces), out_shape=(pltpu.VMEM((f...  2.53 us
    ppermute x1, waiting for transfers between devices, per_device(): lax.ppermute(away, 'section', list(enumerate(route))).astype(jnp.float32)  1.97 us
    ppermute x1, starting transfers between devices, per_device(): lax.ppermute(away, 'section', list(enumerate(route))).astype(jnp.float32)  1.54 us
    ppermute x1, starting transfers between devices, per_device(): own = own + lax.ppermute(near, SHARDS, pairs).astype(jnp.float32)  1.34 us
    ppermute x4, waiting for transfers between devices, per_device(): lax.ppermute(query, ('half', 'dp'), [(n * h + i, n * (h if i != t else 1...  1.28 us
    ppermute x2, waiting for transfers between devices, across(): return lax.ppermute(x, 'half', [(0, 1), (1, 0)])  1.09 us
    pallas_call x1, Pallas kernels, per_device(): pl.pallas_call(functools.partial(local_scores, n, len(blocks), routes), o...  0.84 us
  transfers between devices with their start and end apart: 8, of which 5 were waited for; matrix products, arithmetic and copies ran while one was open for 0% of the time, Pallas kernels for 15%

profile of v6, /device:TPU:0, one launch (start us, length us, event | category | flops | bytes accessed | tf_op | source)
XLA Modules:
  0.0 17.3 jit_solution(744651683960447915)
XLA Ops:
  0.0 0.0 copy-start
  0.0 3.0 %collective-permute-start = (bf16[16,1536]{1,0:T(8,128)(2,1)}, bf16[16,1536]{1,0:T(8,128)(2,1)S(1)}, u32[]{:S(2)}, u32[]{:S(2)}) collective-permute-start(bf16[16,1536]{1,0:T(8,128)(2,1)} %refs_0_.1), channel_id=1, source_target_pairs={{0,1},{1,3},{2,6},{3,0},{4,5},{5,7},{6,2},{7,4},{8,9},{9,11},{10,1... | collective-permute-start | bytes 147464 | tf_op jit(solution)/shard_map/ppermute | solution.py:91
  3.0 1.1 %collective-permute-start.1 = (bf16[16,1536]{1,0:T(8,128)(2,1)}, bf16[16,1536]{1,0:T(8,128)(2,1)S(1)}, u32[]{:S(2)}, u32[]{:S(2)}) collective-permute-start(bf16[16,1536]{1,0:T(8,128)(2,1)} %refs_0_.1), channel_id=1, source_target_pairs={{0,2},{1,5},{2,0},{3,7},{4,6},{5,1},{6,4},{7,3},{8,10},{9,13},{10,... | collective-permute-start | bytes 147464 | tf_op jit(solution)/shard_map/ppermute | solution.py:91
  4.1 1.1 %collective-permute-start.2 = (bf16[16,1536]{1,0:T(8,128)(2,1)}, bf16[16,1536]{1,0:T(8,128)(2,1)S(1)}, u32[]{:S(2)}, u32[]{:S(2)}) collective-permute-start(bf16[16,1536]{1,0:T(8,128)(2,1)} %refs_0_.1), channel_id=1, source_target_pairs={{0,3},{1,0},{2,1},{3,2},{4,7},{5,4},{6,5},{7,6},{8,11},{9,8},{10,9... | collective-permute-start | bytes 147464 | tf_op jit(solution)/shard_map/ppermute | solution.py:91
  5.2 0.2 collective-permute-start.3
  5.3 2.5 %stage.1 = (bf16[1536,1024]{1,0:T(8,128)(2,1)S(1)}, bf16[6,256,256]{2,1,0:T(8,128)(2,1)S(1)}, f32[6,1,256]{2,1,0:T(1,128)S(1)}) custom-call(bf16[1024,1536]{1,0:T(8,128)(2,1)} %train.1, bf16[6,256,256]{2,1,0:T(8,128)(2,1)} %precond.1, s32[6]{0:T(128)} %kind.1, f32[7]{0:T(128)} %scale.1), custom_call_target="tpu_custom_call" | custom-call | bytes 6291456 | tf_op jit(solution)/shard_map/stage/pallas_call | solution.py:99
  7.9 0.0 collective-permute-done.refs_1_
  7.9 0.4 %collective-permute-done.1.refs_2_ = bf16[16,1536]{1,0:T(8,128)(2,1)S(1)} collective-permute-done((bf16[16,1536]{1,0:T(8,128)(2,1)}, bf16[16,1536]{1,0:T(8,128)(2,1)S(1)}, u32[]{:S(2)}, u32[]{:S(2)}) %collective-permute-start.1) | collective-permute-done | bytes 49184 | tf_op jit(solution)/shard_map/ppermute | solution.py:91
  8.3 0.9 %collective-permute-done.2.refs_3_ = bf16[16,1536]{1,0:T(8,128)(2,1)S(1)} collective-permute-done((bf16[16,1536]{1,0:T(8,128)(2,1)}, bf16[16,1536]{1,0:T(8,128)(2,1)S(1)}, u32[]{:S(2)}, u32[]{:S(2)}) %collective-permute-start.2) | collective-permute-done | bytes 49184 | tf_op jit(solution)/shard_map/ppermute | solution.py:91
  9.2 0.0 collective-permute-done.3.refs_4_
  9.2 0.0 copy-done
  9.2 0.8 %local_scores.1 = (f32[16,1024]{1,0:T(8,128)S(1)}, f32[16,1024]{1,0:T(8,128)S(1)}, f32[16,1024]{1,0:T(8,128)S(1)}, bf16[16,1024]{1,0:T(8,128)(2,1)S(1)}) custom-call(bf16[16,1536]{1,0:T(8,128)(2,1)S(1)} %copy-done, bf16[16,1536]{1,0:T(8,128)(2,1)S(1)} %collective-permute-done.refs_1_, bf16[16,1536]{1,0:T(8,128)(2,1)S(1)} %collective-permute-done.1.refs_2_, ...), custom_call_target="tpu_custom_call" | custom-call | tf_op jit(solution)/shard_map/local_scores/pallas_call | solution.py:122
  10.0 0.1 collective-permute-start.5
  10.1 1.5 %collective-permute-start.4 = (bf16[16,1024]{1,0:T(8,128)(2,1)S(1)}, bf16[16,1024]{1,0:T(8,128)(2,1)S(1)}, u32[]{:S(2)}, u32[]{:S(2)}) collective-permute-start(bf16[16,1024]{1,0:T(8,128)(2,1)S(1)} %get-tuple-element.16), channel_id=1, source_target_pairs={{0,8},{8,16},{16,24},{24,0},{1,9},{9,17},{17,25},{25,1},{2,10},{10... | collective-permute-start | bytes 98312 | tf_op jit(solution)/shard_map/ppermute | solution.py:137
  11.6 0.0 collective-permute-done.5
  11.7 1.3 %collective-permute-start.6 = (bf16[16,1024]{1,0:T(8,128)(2,1)S(1)}, bf16[16,1024]{1,0:T(8,128)(2,1)S(1)}, u32[]{:S(2)}, u32[]{:S(2)}) collective-permute-start(bf16[16,1024]{1,0:T(8,128)(2,1)S(1)} %add_convert_fusion), channel_id=1, source_target_pairs={{0,20},{4,24},{8,28},{12,0},{16,4},{20,8},{24,12},{28,16},{1,21},{... | collective-permute-start | bytes 98312 | tf_op jit(solution)/shard_map/ppermute | solution.py:139
  13.0 2.0 %collective-permute-done.4 = bf16[16,1024]{1,0:T(8,128)(2,1)S(1)} collective-permute-done((bf16[16,1024]{1,0:T(8,128)(2,1)S(1)}, bf16[16,1024]{1,0:T(8,128)(2,1)S(1)}, u32[]{:S(2)}, u32[]{:S(2)}) %collective-permute-start.4) | collective-permute-done | bytes 32800 | tf_op jit(solution)/shard_map/ppermute | solution.py:137
  15.0 0.4 %collective-permute-done.6 = bf16[16,1024]{1,0:T(8,128)(2,1)S(1)} collective-permute-done((bf16[16,1024]{1,0:T(8,128)(2,1)S(1)}, bf16[16,1024]{1,0:T(8,128)(2,1)S(1)}, u32[]{:S(2)}, u32[]{:S(2)}) %collective-permute-start.6) | collective-permute-done | bytes 32800 | tf_op jit(solution)/shard_map/ppermute | solution.py:139
  15.4 0.2 %collective-permute-start.7 = (f32[8,1024]{1,0:T(8,128)S(1)}, f32[8,1024]{1,0:T(8,128)S(1)}, u32[]{:S(2)}, u32[]{:S(2)}) collective-permute-start(f32[8,1024]{1,0:T(8,128)S(1)} %slice_select_fusion), channel_id=1, source_target_pairs={{0,4},{4,0},{1,5},{5,1},{2,6},{6,2},{3,7},{7,3},{8,12},{12,8},{9,1... | collective-permute-start | bytes 98312 | tf_op jit(solution)/shard_map/ppermute | solution.py:133
  15.6 1.1 %collective-permute-done.7 = f32[8,1024]{1,0:T(8,128)S(1)} collective-permute-done((f32[8,1024]{1,0:T(8,128)S(1)}, f32[8,1024]{1,0:T(8,128)S(1)}, u32[]{:S(2)}, u32[]{:S(2)}) %collective-permute-start.7) | collective-permute-done | bytes 32800 | tf_op jit(solution)/shard_map/ppermute | solution.py:133
  16.7 0.6 %select_add_fusion = f32[8,1024]{1,0:T(8,128)} fusion(f32[8,1024]{1,0:T(8,128)S(1)} %collective-permute-done.7, f32[16,1024]{1,0:T(8,128)S(1)} %convert_add_fusion, pred[]{:T(512)S(6)} %eq.3), kind=kLoop, calls=%fused_computation.2 | loop fusion | flops 16384 | bytes 131073 | tf_op jit(solution)/shard_map/add | solution.py:143
  (3 shorter events, 0.0 us)
Async XLA Ops:
  0.0 9.2 %copy-start = (bf16[16,1536]{1,0:T(8,128)(2,1)S(1)}, bf16[16,1536]{1,0:T(8,128)(2,1)}, u32[]{:S(2)}) copy-start(bf16[16,1536]{1,0:T(8,128)(2,1)} %refs_0_.1) | copy-start | bytes 147460
  0.0 7.9 %collective-permute-start = (bf16[16,1536]{1,0:T(8,128)(2,1)}, bf16[16,1536]{1,0:T(8,128)(2,1)S(1)}, u32[]{:S(2)}, u32[]{:S(2)}) collective-permute-start(bf16[16,1536]{1,0:T(8,128)(2,1)} %refs_0_.1), channel_id=1, source_target_pairs={{0,1},{1,3},{2,6},{3,0},{4,5},{5,7},{6,2},{7,4},{8,9},{9,11},{10,1... | collective-permute-start | bytes 147464 | tf_op jit(solution)/shard_map/ppermute | solution.py:91
  3.0 5.3 %collective-permute-start.1 = (bf16[16,1536]{1,0:T(8,128)(2,1)}, bf16[16,1536]{1,0:T(8,128)(2,1)S(1)}, u32[]{:S(2)}, u32[]{:S(2)}) collective-permute-start(bf16[16,1536]{1,0:T(8,128)(2,1)} %refs_0_.1), channel_id=1, source_target_pairs={{0,2},{1,5},{2,0},{3,7},{4,6},{5,1},{6,4},{7,3},{8,10},{9,13},{10,... | collective-permute-start | bytes 147464 | tf_op jit(solution)/shard_map/ppermute | solution.py:91
  4.1 5.1 %collective-permute-start.2 = (bf16[16,1536]{1,0:T(8,128)(2,1)}, bf16[16,1536]{1,0:T(8,128)(2,1)S(1)}, u32[]{:S(2)}, u32[]{:S(2)}) collective-permute-start(bf16[16,1536]{1,0:T(8,128)(2,1)} %refs_0_.1), channel_id=1, source_target_pairs={{0,3},{1,0},{2,1},{3,2},{4,7},{5,4},{6,5},{7,6},{8,11},{9,8},{10,9... | collective-permute-start | bytes 147464 | tf_op jit(solution)/shard_map/ppermute | solution.py:91
  5.2 4.0 %collective-permute-start.3 = (bf16[16,1536]{1,0:T(8,128)(2,1)}, bf16[16,1536]{1,0:T(8,128)(2,1)S(1)}, u32[]{:S(2)}, u32[]{:S(2)}) collective-permute-start(bf16[16,1536]{1,0:T(8,128)(2,1)} %refs_0_.1), channel_id=1, source_target_pairs={{0,4},{1,2},{2,3},{3,1},{4,0},{5,6},{6,7},{7,5},{8,12},{9,10},{10,... | collective-permute-start | bytes 147464 | tf_op jit(solution)/shard_map/ppermute | solution.py:91
  10.0 1.6 %collective-permute-start.5 = (f32[16,1024]{1,0:T(8,128)S(1)}, f32[16,1024]{1,0:T(8,128)S(1)}, u32[]{:S(2)}, u32[]{:S(2)}) collective-permute-start(f32[16,1024]{1,0:T(8,128)S(1)} %get-tuple-element.18), channel_id=1, source_target_pairs={{0,4},{4,0},{1,5},{5,1},{2,6},{6,2},{3,7},{7,3},{8,12},{12,8},{9,1... | collective-permute-start | bytes 196616 | tf_op jit(solution)/shard_map/ppermute | solution.py:133
  10.1 4.9 %collective-permute-start.4 = (bf16[16,1024]{1,0:T(8,128)(2,1)S(1)}, bf16[16,1024]{1,0:T(8,128)(2,1)S(1)}, u32[]{:S(2)}, u32[]{:S(2)}) collective-permute-start(bf16[16,1024]{1,0:T(8,128)(2,1)S(1)} %get-tuple-element.16), channel_id=1, source_target_pairs={{0,8},{8,16},{16,24},{24,0},{1,9},{9,17},{17,25},{25,1},{2,10},{10... | collective-permute-start | bytes 98312 | tf_op jit(solution)/shard_map/ppermute | solution.py:137
  11.7 3.7 %collective-permute-start.6 = (bf16[16,1024]{1,0:T(8,128)(2,1)S(1)}, bf16[16,1024]{1,0:T(8,128)(2,1)S(1)}, u32[]{:S(2)}, u32[]{:S(2)}) collective-permute-start(bf16[16,1024]{1,0:T(8,128)(2,1)S(1)} %add_convert_fusion), channel_id=1, source_target_pairs={{0,20},{4,24},{8,28},{12,0},{16,4},{20,8},{24,12},{28,16},{1,21},{... | collective-permute-start | bytes 98312 | tf_op jit(solution)/shard_map/ppermute | solution.py:139
  15.4 1.3 %collective-permute-start.7 = (f32[8,1024]{1,0:T(8,128)S(1)}, f32[8,1024]{1,0:T(8,128)S(1)}, u32[]{:S(2)}, u32[]{:S(2)}) collective-permute-start(f32[8,1024]{1,0:T(8,128)S(1)} %slice_select_fusion), channel_id=1, source_target_pairs={{0,4},{4,0},{1,5},{5,1},{2,6},{6,2},{3,7},{7,3},{8,12},{12,8},{9,1... | collective-permute-start | bytes 98312 | tf_op jit(solution)/shard_map/ppermute | solution.py:133

commit v7 on v6

--- a/solution.py
+++ b/solution.py
@@ -9,9 +9,10 @@
 
 SHARDS = ("section", "half")
 DIRECT = 4
+EARLY = 2
 ROWS = 64
 SHUFFLES = ((1, 3, 2, 0), (2, 1, 0, 3), (3, 0, 1, 2), (0, 2, 3, 1))
-ROUTES = ((2, 3, 0, 1), (3, 0, 1, 2), (1, 2, 3, 0))
+ROUTES = ((3, 2, 0, 1), (1, 0, 3, 2), (2, 3, 1, 0))
 
 
 def stage(pieces, train, precond, kind, scale, train_t, precond_v, factor, raw, kind_s, scale_s, sems):
@@ -38,6 +39,45 @@
         pre = jnp.dot(lhs[:, m * feat:(m + 1) * feat], precond[m], preferred_element_type=jnp.float32)
         parts.append((pre * factor[m]).astype(jnp.bfloat16))
     return jnp.dot(jnp.concatenate(parts, axis=1), train_t[...], preferred_element_type=jnp.float32)
+
+
+def destinations(routes):
+    section, half = lax.axis_index("section"), lax.axis_index("half")
+    to = [sum(jnp.where(section == source, target, 0) for source, target in enumerate(route)) for route in routes]
+    return (section, jnp.where(half == 0, to[0], to[1]), jnp.where(half == 0, to[1], to[0]), *to[2:])
+
+
+def sender(shuffle):
+    dp = lax.axis_index("dp")
+    return sum(jnp.where(dp == target, source, 0) for source, target in enumerate(shuffle))
+
+
+def early_scores(routes, *refs):
+    blocks, (train_t, precond, factor, out) = refs[:1 + EARLY], refs[1 + EARLY:]
+    homes, rows = destinations(routes), blocks[0].shape[0]
+    scores = weighted_scores(jnp.concatenate([b[...] for b in blocks], axis=0), train_t, precond, factor)
+    owners = [lax.axis_index("dp")] + [sender(s) for s in SHUFFLES[:EARLY]]
+    for i in reversed(range(1 + EARLY)):
+        place = sum(jnp.where(owners[i] == home, k, 0) for k, home in enumerate(homes))
+        out[place] = scores[i * rows:(i + 1) * rows]
+
+
+def late_scores(routes, *refs):
+    count = len(SHUFFLES) - EARLY
+    blocks, (train_t, precond, factor, early, out) = refs[:count], refs[count:]
+    homes, rows, dp = destinations(routes), blocks[0].shape[0], lax.axis_index("dp")
+    owners = [sender(s) for s in SHUFFLES[EARLY:]]
+
+    def add(used):
+        scores = weighted_scores(jnp.concatenate([b[...] for b in blocks[:used]], axis=0), train_t, precond, factor)
+        for i in range(used):
+            place = sum(jnp.where(owners[i] == home, k, 0) for k, home in enumerate(homes))
+            out[place] = scores[i * rows:(i + 1) * rows]
+
+    out[...] = early[...]
+    idle = owners[-1] == dp
+    pl.when(idle)(lambda: add(count - 1))
+    pl.when(jnp.logical_not(idle))(lambda: add(count))
 
 
 def local_scores(n, blocks_in, routes, *refs):
@@ -119,15 +159,38 @@
     far = routes[2:]
     shape = (own_rows, cols)
     whole, half_width = jax.ShapeDtypeStruct(shape, jnp.float32), jax.ShapeDtypeStruct(shape, jnp.bfloat16)
-    own, near, swap, *aways = pl.pallas_call(
-        functools.partial(local_scores, n, len(blocks), routes),
-        out_shape=(whole, whole, whole) + (half_width,) * len(far),
-        in_specs=[vmem] * (len(blocks) + 3),
-        out_specs=(vmem,) * (3 + len(far)),
-        scratch_shapes=[pltpu.VMEM((n * query.shape[0], feats), query.dtype)],
-        compiler_params=pltpu.CompilerParams(vmem_limit_bytes=48 * 2**20),
-        name="local_scores",
-    )(*blocks, *staged)
+    params = pltpu.CompilerParams(vmem_limit_bytes=48 * 2**20)
+    if direct:
+        part = jax.ShapeDtypeStruct((sections, *shape), jnp.float32)
+        early, late = blocks[:1 + EARLY], blocks[1 + EARLY:]
+        scores = pl.pallas_call(
+            functools.partial(early_scores, routes),
+            out_shape=part,
+            in_specs=[vmem] * (len(early) + 3),
+            out_specs=vmem,
+            compiler_params=params,
+            name="early_scores",
+        )(*early, *staged)
+        scores = pl.pallas_call(
+            functools.partial(late_scores, routes),
+            out_shape=part,
+            in_specs=[vmem] * (len(late) + 4),
+            out_specs=vmem,
+            compiler_params=params,
+            name="late_scores",
+        )(*late, *staged, scores)
+        own, near, swap, *aways = (scores[i] for i in range(sections))
+        aways = [a.astype(jnp.bfloat16) for a in aways]
+    else:
+        own, near, swap, *aways = pl.pallas_call(
+            functools.partial(local_scores, n, len(blocks), routes),
+            out_shape=(whole, whole, whole) + (half_width,) * len(far),
+            in_specs=[vmem] * (len(blocks) + 3),
+            out_specs=(vmem,) * (3 + len(far)),
+            scratch_shapes=[pltpu.VMEM((n * query.shape[0], feats), query.dtype)],
+            compiler_params=pltpu.CompilerParams(vmem_limit_bytes=48 * 2**20),
+            name="local_scores",
+        )(*blocks, *staged)
 
     def across(x):
         return lax.ppermute(x, "half", [(0, 1), (1, 0)])

time: 17.5 us -> 17.4 us (level)
  the two profiles are of different devices: /device:TPU:0 before, /device:TPU:13 now
where the time goes in v7:
time: 17.4 us; the launch traced here: 17.3 us
  starting transfers between devices  8.09 us (46%)
  waiting for transfers between devices  4.26 us (24%)
  Pallas kernels  4.16 us (24%)
  other arithmetic  0.65 us (4%)
    ppermute x4, starting transfers between devices, per_device(): lax.ppermute(query, ('half', 'dp'), [(n * h + i, n * (h if i != t else 1...  4.73 us
    ppermute x1, waiting for transfers between devices, per_device(): own = own + lax.ppermute(near, SHARDS, pairs).astype(jnp.float32)  2.69 us
    pallas_call x1, Pallas kernels, per_device(): pl.pallas_call(functools.partial(stage, pieces), out_shape=(pltpu.VMEM((f...  2.53 us
    ppermute x1, starting transfers between devices, per_device(): own = own + lax.ppermute(near, SHARDS, pairs).astype(jnp.float32)  1.24 us
    ppermute x2, waiting for transfers between devices, across(): return lax.ppermute(x, 'half', [(0, 1), (1, 0)])  1.2 us
    ppermute x1, starting transfers between devices, per_device(): lax.ppermute(away, 'section', list(enumerate(route))).astype(jnp.float32)  1.15 us
    ppermute x2, starting transfers between devices, across(): return lax.ppermute(x, 'half', [(0, 1), (1, 0)])  0.97 us
    pallas_call x1, Pallas kernels, per_device(): pl.pallas_call(functools.partial(late_scores, routes), out_shape=part, in...  0.82 us
  transfers between devices with their start and end apart: 8, of which 3 were waited for; matrix products, arithmetic and copies ran while one was open for 0% of the time, Pallas kernels for 19%

profile of v7, /device:TPU:13, one launch (start us, length us, event | category | flops | bytes accessed | tf_op | source)
XLA Modules:
  0.0 17.3 jit_solution(10566233091143111014)
XLA Ops:
  0.0 0.0 copy-start
  0.0 2.3 %collective-permute-start.2 = (bf16[16,1536]{1,0:T(8,128)(2,1)}, bf16[16,1536]{1,0:T(8,128)(2,1)S(1)}, u32[]{:S(2)}, u32[]{:S(2)}) collective-permute-start(bf16[16,1536]{1,0:T(8,128)(2,1)} %refs_0_.1), channel_id=1, source_target_pairs={{0,1},{1,3},{2,6},{3,0},{4,5},{5,7},{6,2},{7,4},{8,9},{9,11},{10,1... | collective-permute-start | bytes 147464 | tf_op jit(solution)/shard_map/ppermute | solution.py:131
  2.3 1.0 %collective-permute-start.3 = (bf16[16,1536]{1,0:T(8,128)(2,1)}, bf16[16,1536]{1,0:T(8,128)(2,1)S(1)}, u32[]{:S(2)}, u32[]{:S(2)}) collective-permute-start(bf16[16,1536]{1,0:T(8,128)(2,1)} %refs_0_.1), channel_id=1, source_target_pairs={{0,2},{1,5},{2,0},{3,7},{4,6},{5,1},{6,4},{7,3},{8,10},{9,13},{10,... | collective-permute-start | bytes 147464 | tf_op jit(solution)/shard_map/ppermute | solution.py:131
  3.3 0.0 collective-permute-start
  3.3 1.5 %collective-permute-start.1 = (bf16[16,1536]{1,0:T(8,128)(2,1)}, bf16[16,1536]{1,0:T(8,128)(2,1)S(1)}, u32[]{:S(2)}, u32[]{:S(2)}) collective-permute-start(bf16[16,1536]{1,0:T(8,128)(2,1)} %refs_0_.1), channel_id=1, source_target_pairs={{0,4},{1,2},{2,3},{3,1},{4,0},{5,6},{6,7},{7,5},{8,12},{9,10},{10,... | collective-permute-start | bytes 147464 | tf_op jit(solution)/shard_map/ppermute | solution.py:131
  4.7 2.5 %stage.1 = (bf16[1536,1024]{1,0:T(8,128)(2,1)S(1)}, bf16[6,256,256]{2,1,0:T(8,128)(2,1)S(1)}, f32[6,1,256]{2,1,0:T(1,128)S(1)}) custom-call(bf16[1024,1536]{1,0:T(8,128)(2,1)} %train.1, bf16[6,256,256]{2,1,0:T(8,128)(2,1)} %precond.1, s32[6]{0:T(128)} %kind.1, f32[7]{0:T(128)} %scale.1), custom_call_target="tpu_custom_call" | custom-call | bytes 6291456 | tf_op jit(solution)/shard_map/stage/pallas_call | solution.py:139
  7.3 0.0 collective-permute-done.2.refs_1_
  7.3 0.0 collective-permute-done.3.refs_2_
  7.3 0.0 copy-done
  7.3 0.8 %early_scores.1.refs_5_ = f32[4,16,1024]{2,1,0:T(8,128)S(1)} custom-call(bf16[16,1536]{1,0:T(8,128)(2,1)S(1)} %copy-done, bf16[16,1536]{1,0:T(8,128)(2,1)S(1)} %collective-permute-done.2.refs_1_, bf16[16,1536]{1,0:T(8,128)(2,1)S(1)} %collective-permute-done.3.refs_2_, bf16[1536,1024]{1,0:T(8,128)(2,1)S(1)} %get-tuple-element.8.refs_3_.refs_2_, ...), custom_call_target="tpu_custom_call" | custom-call | tf_op jit(solution)/shard_map/early_scores/pallas_call | solution.py:166
  8.1 0.0 collective-permute-done.refs_0_
  8.1 0.0 collective-permute-done.1.refs_1_
  8.1 0.8 %late_scores.1 = f32[4,16,1024]{2,1,0:T(8,128)S(1)} custom-call(bf16[16,1536]{1,0:T(8,128)(2,1)S(1)} %collective-permute-done.refs_0_, bf16[16,1536]{1,0:T(8,128)(2,1)S(1)} %collective-permute-done.1.refs_1_, bf16[1536,1024]{1,0:T(8,128)(2,1)S(1)} %get-tuple-element.8.refs_3_.refs_2_, bf16[6,256,256]{2,1,0:T(8,128)(2,1)S(1)} %get-tuple-element.9.refs_4_.refs_3_, ...), custom_call_target="tpu_custom_call" | custom-call | tf_op jit(solution)/shard_map/late_scores/pallas_call | solution.py:174
  9.0 0.9 %collective-permute-start.5 = (f32[16,1024]{1,0:T(8,128)S(1)}, f32[16,1024]{1,0:T(8,128)S(1)}, u32[]{:S(2)}, u32[]{:S(2)}) collective-permute-start(f32[16,1024]{1,0:T(8,128)S(1)} %slice_bitcast_fusion), channel_id=1, source_target_pairs={{0,4},{4,0},{1,5},{5,1},{2,6},{6,2},{3,7},{7,3},{8,12},{12,8},{9,1... | collective-permute-start | bytes 196616 | tf_op jit(solution)/shard_map/ppermute | solution.py:196
  9.9 1.2 %collective-permute-start.4 = (bf16[16,1024]{1,0:T(8,128)(2,1)S(1)}, bf16[16,1024]{1,0:T(8,128)(2,1)S(1)}, u32[]{:S(2)}, u32[]{:S(2)}) collective-permute-start(bf16[16,1024]{1,0:T(8,128)(2,1)S(1)} %fusion.4), channel_id=1, source_target_pairs={{0,16},{8,24},{16,8},{24,0},{1,17},{9,25},{17,9},{25,1},{2,18},{10... | collective-permute-start | bytes 98312 | tf_op jit(solution)/shard_map/ppermute | solution.py:200
  11.0 0.0 collective-permute-done.5
  11.1 1.2 %collective-permute-start.6 = (bf16[16,1024]{1,0:T(8,128)(2,1)S(1)}, bf16[16,1024]{1,0:T(8,128)(2,1)S(1)}, u32[]{:S(2)}, u32[]{:S(2)}) collective-permute-start(bf16[16,1024]{1,0:T(8,128)(2,1)S(1)} %fusion.1), channel_id=1, source_target_pairs={{0,28},{4,8},{8,20},{12,0},{16,4},{20,24},{24,12},{28,16},{1,29},{... | collective-permute-start | bytes 98312 | tf_op jit(solution)/shard_map/ppermute | solution.py:202
  12.3 0.4 %collective-permute-done.4 = bf16[16,1024]{1,0:T(8,128)(2,1)S(1)} collective-permute-done((bf16[16,1024]{1,0:T(8,128)(2,1)S(1)}, bf16[16,1024]{1,0:T(8,128)(2,1)S(1)}, u32[]{:S(2)}, u32[]{:S(2)}) %collective-permute-start.4) | collective-permute-done | bytes 32800 | tf_op jit(solution)/shard_map/ppermute | solution.py:200
  12.6 2.7 %collective-permute-done.6 = bf16[16,1024]{1,0:T(8,128)(2,1)S(1)} collective-permute-done((bf16[16,1024]{1,0:T(8,128)(2,1)S(1)}, bf16[16,1024]{1,0:T(8,128)(2,1)S(1)}, u32[]{:S(2)}, u32[]{:S(2)}) %collective-permute-start.6) | collective-permute-done | bytes 32800 | tf_op jit(solution)/shard_map/ppermute | solution.py:202
  15.4 0.1 collective-permute-start.7
  15.5 1.2 %collective-permute-done.7 = f32[8,1024]{1,0:T(8,128)S(1)} collective-permute-done((f32[8,1024]{1,0:T(8,128)S(1)}, f32[8,1024]{1,0:T(8,128)S(1)}, u32[]{:S(2)}, u32[]{:S(2)}) %collective-permute-start.7) | collective-permute-done | bytes 32800 | tf_op jit(solution)/shard_map/ppermute | solution.py:196
  16.6 0.6 %select_add_fusion = f32[8,1024]{1,0:T(8,128)} fusion(f32[8,1024]{1,0:T(8,128)S(1)} %collective-permute-done.7, f32[16,1024]{1,0:T(8,128)S(1)} %fusion.3, pred[]{:T(512)S(6)} %eq.3), kind=kLoop, calls=%fused_computation.9 | loop fusion | flops 16384 | bytes 131073 | tf_op jit(solution)/shard_map/add | solution.py:206
  (5 shorter events, 0.0 us)
Async XLA Ops:
  0.0 7.3 %copy-start = (bf16[16,1536]{1,0:T(8,128)(2,1)S(1)}, bf16[16,1536]{1,0:T(8,128)(2,1)}, u32[]{:S(2)}) copy-start(bf16[16,1536]{1,0:T(8,128)(2,1)} %refs_0_.1) | copy-start | bytes 147460
  0.0 7.3 %collective-permute-start.2 = (bf16[16,1536]{1,0:T(8,128)(2,1)}, bf16[16,1536]{1,0:T(8,128)(2,1)S(1)}, u32[]{:S(2)}, u32[]{:S(2)}) collective-permute-start(bf16[16,1536]{1,0:T(8,128)(2,1)} %refs_0_.1), channel_id=1, source_target_pairs={{0,1},{1,3},{2,6},{3,0},{4,5},{5,7},{6,2},{7,4},{8,9},{9,11},{10,1... | collective-permute-start | bytes 147464 | tf_op jit(solution)/shard_map/ppermute | solution.py:131
  2.3 5.0 %collective-permute-start.3 = (bf16[16,1536]{1,0:T(8,128)(2,1)}, bf16[16,1536]{1,0:T(8,128)(2,1)S(1)}, u32[]{:S(2)}, u32[]{:S(2)}) collective-permute-start(bf16[16,1536]{1,0:T(8,128)(2,1)} %refs_0_.1), channel_id=1, source_target_pairs={{0,2},{1,5},{2,0},{3,7},{4,6},{5,1},{6,4},{7,3},{8,10},{9,13},{10,... | collective-permute-start | bytes 147464 | tf_op jit(solution)/shard_map/ppermute | solution.py:131
  3.3 4.9 %collective-permute-start = (bf16[16,1536]{1,0:T(8,128)(2,1)}, bf16[16,1536]{1,0:T(8,128)(2,1)S(1)}, u32[]{:S(2)}, u32[]{:S(2)}) collective-permute-start(bf16[16,1536]{1,0:T(8,128)(2,1)} %refs_0_.1), channel_id=1, source_target_pairs={{0,3},{1,0},{2,1},{3,2},{4,7},{5,4},{6,5},{7,6},{8,11},{9,8},{10,9... | collective-permute-start | bytes 147464 | tf_op jit(solution)/shard_map/ppermute | solution.py:131
  3.3 4.9 %collective-permute-start.1 = (bf16[16,1536]{1,0:T(8,128)(2,1)}, bf16[16,1536]{1,0:T(8,128)(2,1)S(1)}, u32[]{:S(2)}, u32[]{:S(2)}) collective-permute-start(bf16[16,1536]{1,0:T(8,128)(2,1)} %refs_0_.1), channel_id=1, source_target_pairs={{0,4},{1,2},{2,3},{3,1},{4,0},{5,6},{6,7},{7,5},{8,12},{9,10},{10,... | collective-permute-start | bytes 147464 | tf_op jit(solution)/shard_map/ppermute | solution.py:131
  9.0 2.1 %collective-permute-start.5 = (f32[16,1024]{1,0:T(8,128)S(1)}, f32[16,1024]{1,0:T(8,128)S(1)}, u32[]{:S(2)}, u32[]{:S(2)}) collective-permute-start(f32[16,1024]{1,0:T(8,128)S(1)} %slice_bitcast_fusion), channel_id=1, source_target_pairs={{0,4},{4,0},{1,5},{5,1},{2,6},{6,2},{3,7},{7,3},{8,12},{12,8},{9,1... | collective-permute-start | bytes 196616 | tf_op jit(solution)/shard_map/ppermute | solution.py:196
  9.9 2.8 %collective-permute-start.4 = (bf16[16,1024]{1,0:T(8,128)(2,1)S(1)}, bf16[16,1024]{1,0:T(8,128)(2,1)S(1)}, u32[]{:S(2)}, u32[]{:S(2)}) collective-permute-start(bf16[16,1024]{1,0:T(8,128)(2,1)S(1)} %fusion.4), channel_id=1, source_target_pairs={{0,16},{8,24},{16,8},{24,0},{1,17},{9,25},{17,9},{25,1},{2,18},{10... | collective-permute-start | bytes 98312 | tf_op jit(solution)/shard_map/ppermute | solution.py:200
  11.1 4.3 %collective-permute-start.6 = (bf16[16,1024]{1,0:T(8,128)(2,1)S(1)}, bf16[16,1024]{1,0:T(8,128)(2,1)S(1)}, u32[]{:S(2)}, u32[]{:S(2)}) collective-permute-start(bf16[16,1024]{1,0:T(8,128)(2,1)S(1)} %fusion.1), channel_id=1, source_target_pairs={{0,28},{4,8},{8,20},{12,0},{16,4},{20,24},{24,12},{28,16},{1,29},{... | collective-permute-start | bytes 98312 | tf_op jit(solution)/shard_map/ppermute | solution.py:202
  15.4 1.3 %collective-permute-start.7 = (f32[8,1024]{1,0:T(8,128)S(1)}, f32[8,1024]{1,0:T(8,128)S(1)}, u32[]{:S(2)}, u32[]{:S(2)}) collective-permute-start(f32[8,1024]{1,0:T(8,128)S(1)} %slice_select_fusion), channel_id=1, source_target_pairs={{0,4},{4,0},{1,5},{5,1},{2,6},{6,2},{3,7},{7,3},{8,12},{12,8},{9,1... | collective-permute-start | bytes 98312 | tf_op jit(solution)/shard_map/ppermute | solution.py:196

commit v8 on v7

--- a/solution.py
+++ b/solution.py
@@ -197,7 +197,8 @@
 
     near = (near + across(swap)).astype(jnp.bfloat16)
     for route, away in zip(far, aways):
-        own = own + lax.ppermute(away, "section", list(enumerate(route))).astype(jnp.float32)
+        crossed = [(2 * i + h, 2 * t + 1 - h) for i, t in enumerate(route) for h in range(2)]
+        own = own + lax.ppermute(away, SHARDS, crossed).astype(jnp.float32)
     pairs = [(2 * i + h, 2 * routes[h][i] + 1 - h) for i in range(sections) for h in range(2)]
     own = own + lax.ppermute(near, SHARDS, pairs).astype(jnp.float32)
     rows = own_rows // 2

time: 17.4 us -> 17.4 us (level)
    ppermute x1, waiting for transfers between devices: 2.69 us -> 2.08 us  [per_device(): own = own + lax.ppermute(near, SHARDS, pairs).astype(jnp.float32)]
    ppermute x1, waiting for transfers between devices: 0.36 us -> 0.93 us  [per_device(): own = own + lax.ppermute(away, SHARDS, crossed).astype(jnp.float32)]
where the time goes in v8:
time: 17.4 us; the launch traced here: 17.2 us
  starting transfers between devices  8.09 us (46%)
  waiting for transfers between devices  4.22 us (24%)
  Pallas kernels  4.16 us (24%)
  other arithmetic  0.65 us (4%)
    ppermute x4, starting transfers between devices, per_device(): lax.ppermute(query, ('half', 'dp'), [(n * h + i, n * (h if i != t else 1...  4.73 us
    pallas_call x1, Pallas kernels, per_device(): pl.pallas_call(functools.partial(stage, pieces), out_shape=(pltpu.VMEM((f...  2.53 us
    ppermute x1, waiting for transfers between devices, per_device(): own = own + lax.ppermute(near, SHARDS, pairs).astype(jnp.float32)  2.08 us
    ppermute x1, starting transfers between devices, per_device(): own = own + lax.ppermute(near, SHARDS, pairs).astype(jnp.float32)  1.28 us
    ppermute x2, waiting for transfers between devices, across(): return lax.ppermute(x, 'half', [(0, 1), (1, 0)])  1.2 us
    ppermute x1, starting transfers between devices, per_device(): own = own + lax.ppermute(away, SHARDS, crossed).astype(jnp.float32)  1.11 us
    ppermute x2, starting transfers between devices, across(): return lax.ppermute(x, 'half', [(0, 1), (1, 0)])  0.97 us
    ppermute x1, waiting for transfers between devices, per_device(): own = own + lax.ppermute(away, SHARDS, crossed).astype(jnp.float32)  0.93 us
  transfers between devices with their start and end apart: 8, of which 3 were waited for; matrix products, arithmetic and copies ran while one was open for 0% of the time, Pallas kernels for 19%

profile of v8, /device:TPU:13, one launch (start us, length us, event | category | flops | bytes accessed | tf_op | source)
XLA Modules:
  0.0 17.2 jit_solution(17815765975650001522)
XLA Ops:
  0.0 0.0 copy-start
  0.0 2.3 %collective-permute-start.2 = (bf16[16,1536]{1,0:T(8,128)(2,1)}, bf16[16,1536]{1,0:T(8,128)(2,1)S(1)}, u32[]{:S(2)}, u32[]{:S(2)}) collective-permute-start(bf16[16,1536]{1,0:T(8,128)(2,1)} %refs_0_.1), channel_id=1, source_target_pairs={{0,1},{1,3},{2,6},{3,0},{4,5},{5,7},{6,2},{7,4},{8,9},{9,11},{10,1... | collective-permute-start | bytes 147464 | tf_op jit(solution)/shard_map/ppermute | solution.py:131
  2.3 1.0 %collective-permute-start.3 = (bf16[16,1536]{1,0:T(8,128)(2,1)}, bf16[16,1536]{1,0:T(8,128)(2,1)S(1)}, u32[]{:S(2)}, u32[]{:S(2)}) collective-permute-start(bf16[16,1536]{1,0:T(8,128)(2,1)} %refs_0_.1), channel_id=1, source_target_pairs={{0,2},{1,5},{2,0},{3,7},{4,6},{5,1},{6,4},{7,3},{8,10},{9,13},{10,... | collective-permute-start | bytes 147464 | tf_op jit(solution)/shard_map/ppermute | solution.py:131
  3.3 0.0 collective-permute-start
  3.3 1.5 %collective-permute-start.1 = (bf16[16,1536]{1,0:T(8,128)(2,1)}, bf16[16,1536]{1,0:T(8,128)(2,1)S(1)}, u32[]{:S(2)}, u32[]{:S(2)}) collective-permute-start(bf16[16,1536]{1,0:T(8,128)(2,1)} %refs_0_.1), channel_id=1, source_target_pairs={{0,4},{1,2},{2,3},{3,1},{4,0},{5,6},{6,7},{7,5},{8,12},{9,10},{10,... | collective-permute-start | bytes 147464 | tf_op jit(solution)/shard_map/ppermute | solution.py:131
  4.7 2.5 %stage.1 = (bf16[1536,1024]{1,0:T(8,128)(2,1)S(1)}, bf16[6,256,256]{2,1,0:T(8,128)(2,1)S(1)}, f32[6,1,256]{2,1,0:T(1,128)S(1)}) custom-call(bf16[1024,1536]{1,0:T(8,128)(2,1)} %train.1, bf16[6,256,256]{2,1,0:T(8,128)(2,1)} %precond.1, s32[6]{0:T(128)} %kind.1, f32[7]{0:T(128)} %scale.1), custom_call_target="tpu_custom_call" | custom-call | bytes 6291456 | tf_op jit(solution)/shard_map/stage/pallas_call | solution.py:139
  7.3 0.0 collective-permute-done.2.refs_1_
  7.3 0.0 collective-permute-done.3.refs_2_
  7.3 0.0 copy-done
  7.3 0.8 %early_scores.1.refs_5_ = f32[4,16,1024]{2,1,0:T(8,128)S(1)} custom-call(bf16[16,1536]{1,0:T(8,128)(2,1)S(1)} %copy-done, bf16[16,1536]{1,0:T(8,128)(2,1)S(1)} %collective-permute-done.2.refs_1_, bf16[16,1536]{1,0:T(8,128)(2,1)S(1)} %collective-permute-done.3.refs_2_, bf16[1536,1024]{1,0:T(8,128)(2,1)S(1)} %get-tuple-element.8.refs_3_.refs_2_, ...), custom_call_target="tpu_custom_call" | custom-call | tf_op jit(solution)/shard_map/early_scores/pallas_call | solution.py:166
  8.1 0.0 collective-permute-done.refs_0_
  8.1 0.0 collective-permute-done.1.refs_1_
  8.1 0.8 %late_scores.1 = f32[4,16,1024]{2,1,0:T(8,128)S(1)} custom-call(bf16[16,1536]{1,0:T(8,128)(2,1)S(1)} %collective-permute-done.refs_0_, bf16[16,1536]{1,0:T(8,128)(2,1)S(1)} %collective-permute-done.1.refs_1_, bf16[1536,1024]{1,0:T(8,128)(2,1)S(1)} %get-tuple-element.8.refs_3_.refs_2_, bf16[6,256,256]{2,1,0:T(8,128)(2,1)S(1)} %get-tuple-element.9.refs_4_.refs_3_, ...), custom_call_target="tpu_custom_call" | custom-call | tf_op jit(solution)/shard_map/late_scores/pallas_call | solution.py:174
  9.0 0.9 %collective-permute-start.5 = (f32[16,1024]{1,0:T(8,128)S(1)}, f32[16,1024]{1,0:T(8,128)S(1)}, u32[]{:S(2)}, u32[]{:S(2)}) collective-permute-start(f32[16,1024]{1,0:T(8,128)S(1)} %slice_bitcast_fusion), channel_id=1, source_target_pairs={{0,4},{4,0},{1,5},{5,1},{2,6},{6,2},{3,7},{7,3},{8,12},{12,8},{9,1... | collective-permute-start | bytes 196616 | tf_op jit(solution)/shard_map/ppermute | solution.py:196
  9.9 1.1 %collective-permute-start.4 = (bf16[16,1024]{1,0:T(8,128)(2,1)S(1)}, bf16[16,1024]{1,0:T(8,128)(2,1)S(1)}, u32[]{:S(2)}, u32[]{:S(2)}) collective-permute-start(bf16[16,1024]{1,0:T(8,128)(2,1)S(1)} %fusion.4), channel_id=1, source_target_pairs={{0,20},{4,16},{8,28},{12,24},{16,12},{20,8},{24,4},{28,0},{1,21},{... | collective-permute-start | bytes 98312 | tf_op jit(solution)/shard_map/ppermute | solution.py:201
  11.0 0.0 collective-permute-done.5
  11.0 1.3 %collective-permute-start.6 = (bf16[16,1024]{1,0:T(8,128)(2,1)S(1)}, bf16[16,1024]{1,0:T(8,128)(2,1)S(1)}, u32[]{:S(2)}, u32[]{:S(2)}) collective-permute-start(bf16[16,1024]{1,0:T(8,128)(2,1)S(1)} %fusion.1), channel_id=1, source_target_pairs={{0,28},{4,8},{8,20},{12,0},{16,4},{20,24},{24,12},{28,16},{1,29},{... | collective-permute-start | bytes 98312 | tf_op jit(solution)/shard_map/ppermute | solution.py:203
  12.3 0.9 %collective-permute-done.4 = bf16[16,1024]{1,0:T(8,128)(2,1)S(1)} collective-permute-done((bf16[16,1024]{1,0:T(8,128)(2,1)S(1)}, bf16[16,1024]{1,0:T(8,128)(2,1)S(1)}, u32[]{:S(2)}, u32[]{:S(2)}) %collective-permute-start.4) | collective-permute-done | bytes 32800 | tf_op jit(solution)/shard_map/ppermute | solution.py:201
  13.2 2.1 %collective-permute-done.6 = bf16[16,1024]{1,0:T(8,128)(2,1)S(1)} collective-permute-done((bf16[16,1024]{1,0:T(8,128)(2,1)S(1)}, bf16[16,1024]{1,0:T(8,128)(2,1)S(1)}, u32[]{:S(2)}, u32[]{:S(2)}) %collective-permute-start.6) | collective-permute-done | bytes 32800 | tf_op jit(solution)/shard_map/ppermute | solution.py:203
  15.3 0.1 collective-permute-start.7
  15.4 1.2 %collective-permute-done.7 = f32[8,1024]{1,0:T(8,128)S(1)} collective-permute-done((f32[8,1024]{1,0:T(8,128)S(1)}, f32[8,1024]{1,0:T(8,128)S(1)}, u32[]{:S(2)}, u32[]{:S(2)}) %collective-permute-start.7) | collective-permute-done | bytes 32800 | tf_op jit(solution)/shard_map/ppermute | solution.py:196
  16.6 0.6 %select_add_fusion = f32[8,1024]{1,0:T(8,128)} fusion(f32[8,1024]{1,0:T(8,128)S(1)} %collective-permute-done.7, f32[16,1024]{1,0:T(8,128)S(1)} %fusion.3, pred[]{:T(512)S(6)} %eq.3), kind=kLoop, calls=%fused_computation.9 | loop fusion | flops 16384 | bytes 131073 | tf_op jit(solution)/shard_map/add | solution.py:207
  (5 shorter events, 0.0 us)
Async XLA Ops:
  0.0 7.3 %copy-start = (bf16[16,1536]{1,0:T(8,128)(2,1)S(1)}, bf16[16,1536]{1,0:T(8,128)(2,1)}, u32[]{:S(2)}) copy-start(bf16[16,1536]{1,0:T(8,128)(2,1)} %refs_0_.1) | copy-start | bytes 147460
  0.0 7.3 %collective-permute-start.2 = (bf16[16,1536]{1,0:T(8,128)(2,1)}, bf16[16,1536]{1,0:T(8,128)(2,1)S(1)}, u32[]{:S(2)}, u32[]{:S(2)}) collective-permute-start(bf16[16,1536]{1,0:T(8,128)(2,1)} %refs_0_.1), channel_id=1, source_target_pairs={{0,1},{1,3},{2,6},{3,0},{4,5},{5,7},{6,2},{7,4},{8,9},{9,11},{10,1... | collective-permute-start | bytes 147464 | tf_op jit(solution)/shard_map/ppermute | solution.py:131
  2.3 5.0 %collective-permute-start.3 = (bf16[16,1536]{1,0:T(8,128)(2,1)}, bf16[16,1536]{1,0:T(8,128)(2,1)S(1)}, u32[]{:S(2)}, u32[]{:S(2)}) collective-permute-start(bf16[16,1536]{1,0:T(8,128)(2,1)} %refs_0_.1), channel_id=1, source_target_pairs={{0,2},{1,5},{2,0},{3,7},{4,6},{5,1},{6,4},{7,3},{8,10},{9,13},{10,... | collective-permute-start | bytes 147464 | tf_op jit(solution)/shard_map/ppermute | solution.py:131
  3.3 4.9 %collective-permute-start = (bf16[16,1536]{1,0:T(8,128)(2,1)}, bf16[16,1536]{1,0:T(8,128)(2,1)S(1)}, u32[]{:S(2)}, u32[]{:S(2)}) collective-permute-start(bf16[16,1536]{1,0:T(8,128)(2,1)} %refs_0_.1), channel_id=1, source_target_pairs={{0,3},{1,0},{2,1},{3,2},{4,7},{5,4},{6,5},{7,6},{8,11},{9,8},{10,9... | collective-permute-start | bytes 147464 | tf_op jit(solution)/shard_map/ppermute | solution.py:131
  3.3 4.9 %collective-permute-start.1 = (bf16[16,1536]{1,0:T(8,128)(2,1)}, bf16[16,1536]{1,0:T(8,128)(2,1)S(1)}, u32[]{:S(2)}, u32[]{:S(2)}) collective-permute-start(bf16[16,1536]{1,0:T(8,128)(2,1)} %refs_0_.1), channel_id=1, source_target_pairs={{0,4},{1,2},{2,3},{3,1},{4,0},{5,6},{6,7},{7,5},{8,12},{9,10},{10,... | collective-permute-start | bytes 147464 | tf_op jit(solution)/shard_map/ppermute | solution.py:131
  9.0 2.0 %collective-permute-start.5 = (f32[16,1024]{1,0:T(8,128)S(1)}, f32[16,1024]{1,0:T(8,128)S(1)}, u32[]{:S(2)}, u32[]{:S(2)}) collective-permute-start(f32[16,1024]{1,0:T(8,128)S(1)} %slice_bitcast_fusion), channel_id=1, source_target_pairs={{0,4},{4,0},{1,5},{5,1},{2,6},{6,2},{3,7},{7,3},{8,12},{12,8},{9,1... | collective-permute-start | bytes 196616 | tf_op jit(solution)/shard_map/ppermute | solution.py:196
  9.9 3.3 %collective-permute-start.4 = (bf16[16,1024]{1,0:T(8,128)(2,1)S(1)}, bf16[16,1024]{1,0:T(8,128)(2,1)S(1)}, u32[]{:S(2)}, u32[]{:S(2)}) collective-permute-start(bf16[16,1024]{1,0:T(8,128)(2,1)S(1)} %fusion.4), channel_id=1, source_target_pairs={{0,20},{4,16},{8,28},{12,24},{16,12},{20,8},{24,4},{28,0},{1,21},{... | collective-permute-start | bytes 98312 | tf_op jit(solution)/shard_map/ppermute | solution.py:201
  11.0 4.3 %collective-permute-start.6 = (bf16[16,1024]{1,0:T(8,128)(2,1)S(1)}, bf16[16,1024]{1,0:T(8,128)(2,1)S(1)}, u32[]{:S(2)}, u32[]{:S(2)}) collective-permute-start(bf16[16,1024]{1,0:T(8,128)(2,1)S(1)} %fusion.1), channel_id=1, source_target_pairs={{0,28},{4,8},{8,20},{12,0},{16,4},{20,24},{24,12},{28,16},{1,29},{... | collective-permute-start | bytes 98312 | tf_op jit(solution)/shard_map/ppermute | solution.py:203
  15.3 1.3 %collective-permute-start.7 = (f32[8,1024]{1,0:T(8,128)S(1)}, f32[8,1024]{1,0:T(8,128)S(1)}, u32[]{:S(2)}, u32[]{:S(2)}) collective-permute-start(f32[8,1024]{1,0:T(8,128)S(1)} %slice_select_fusion), channel_id=1, source_target_pairs={{0,4},{4,0},{1,5},{5,1},{2,6},{6,2},{3,7},{7,3},{8,12},{12,8},{9,1... | collective-permute-start | bytes 98312 | tf_op jit(solution)/shard_map/ppermute | solution.py:196

commit v9 on v7

--- a/solution.py
+++ b/solution.py
@@ -135,7 +135,7 @@
         blocks = [lax.all_gather(query, "dp", axis=0, tiled=True)]
 
     vmem, hbm = (pl.BlockSpec(memory_space=s) for s in (pltpu.VMEM, pltpu.HBM))
-    pieces = 4
+    pieces = 8
     staged = pl.pallas_call(
         functools.partial(stage, pieces),
         out_shape=(

time: 17.4 us -> 17.4 us (level)
  Pallas kernels: 4.16 us -> 4.34 us
  starting transfers between devices: 8.09 us -> 7.91 us
    ppermute x2, starting transfers between devices: 0.97 us -> 0.78 us  [across(): return lax.ppermute(x, 'half', [(0, 1), (1, 0)])]
    pallas_call x1, Pallas kernels: 2.53 us -> 2.72 us  [per_device(): pl.pallas_call(functools.partial(stage, pieces), out_shape=(pltpu.VMEM((f...]
  transfers between devices with their start and end apart: 8 -> 8, of which waited for: 3 -> 3; matrix products, arithmetic and copies ran while one was open for 0% -> 0% of each run, Pallas kernels for 19% -> 20%
where the time goes in v9:
time: 17.4 us; the launch traced here: 17.3 us
  starting transfers between devices  7.91 us (45%)
  Pallas kernels  4.34 us (25%)
  waiting for transfers between devices  4.26 us (24%)
  other arithmetic  0.65 us (4%)
    ppermute x4, starting transfers between devices, per_device(): lax.ppermute(query, ('half', 'dp'), [(n * h + i, n * (h if i != t else 1...  4.73 us
    pallas_call x1, Pallas kernels, per_device(): pl.pallas_call(functools.partial(stage, pieces), out_shape=(pltpu.VMEM((f...  2.72 us
    ppermute x1, waiting for transfers between devices, per_device(): own = own + lax.ppermute(near, SHARDS, pairs).astype(jnp.float32)  2.69 us
    ppermute x1, starting transfers between devices, per_device(): own = own + lax.ppermute(near, SHARDS, pairs).astype(jnp.float32)  1.24 us
    ppermute x2, waiting for transfers between devices, across(): return lax.ppermute(x, 'half', [(0, 1), (1, 0)])  1.2 us
    ppermute x1, starting transfers between devices, per_device(): lax.ppermute(away, 'section', list(enumerate(route))).astype(jnp.float32)  1.15 us
    pallas_call x1, Pallas kernels, per_device(): pl.pallas_call(functools.partial(late_scores, routes), out_shape=part, in...  0.82 us
    pallas_call x1, Pallas kernels, per_device(): pl.pallas_call(functools.partial(early_scores, routes), out_shape=part, i...  0.81 us
  transfers between devices with their start and end apart: 8, of which 3 were waited for; matrix products, arithmetic and copies ran while one was open for 0% of the time, Pallas kernels for 20%

profile of v9, /device:TPU:13, one launch (start us, length us, event | category | flops | bytes accessed | tf_op | source)
XLA Modules:
  0.0 17.3 jit_solution(82359177652143341)
XLA Ops:
  0.0 0.0 copy-start
  0.0 2.3 %collective-permute-start.2 = (bf16[16,1536]{1,0:T(8,128)(2,1)}, bf16[16,1536]{1,0:T(8,128)(2,1)S(1)}, u32[]{:S(2)}, u32[]{:S(2)}) collective-permute-start(bf16[16,1536]{1,0:T(8,128)(2,1)} %refs_0_.1), channel_id=1, source_target_pairs={{0,1},{1,3},{2,6},{3,0},{4,5},{5,7},{6,2},{7,4},{8,9},{9,11},{10,1... | collective-permute-start | bytes 147464 | tf_op jit(solution)/shard_map/ppermute | solution.py:131
  2.3 1.0 %collective-permute-start.3 = (bf16[16,1536]{1,0:T(8,128)(2,1)}, bf16[16,1536]{1,0:T(8,128)(2,1)S(1)}, u32[]{:S(2)}, u32[]{:S(2)}) collective-permute-start(bf16[16,1536]{1,0:T(8,128)(2,1)} %refs_0_.1), channel_id=1, source_target_pairs={{0,2},{1,5},{2,0},{3,7},{4,6},{5,1},{6,4},{7,3},{8,10},{9,13},{10,... | collective-permute-start | bytes 147464 | tf_op jit(solution)/shard_map/ppermute | solution.py:131
  3.3 0.0 collective-permute-start
  3.3 1.5 %collective-permute-start.1 = (bf16[16,1536]{1,0:T(8,128)(2,1)}, bf16[16,1536]{1,0:T(8,128)(2,1)S(1)}, u32[]{:S(2)}, u32[]{:S(2)}) collective-permute-start(bf16[16,1536]{1,0:T(8,128)(2,1)} %refs_0_.1), channel_id=1, source_target_pairs={{0,4},{1,2},{2,3},{3,1},{4,0},{5,6},{6,7},{7,5},{8,12},{9,10},{10,... | collective-permute-start | bytes 147464 | tf_op jit(solution)/shard_map/ppermute | solution.py:131
  4.7 2.7 %stage.1 = (bf16[1536,1024]{1,0:T(8,128)(2,1)S(1)}, bf16[6,256,256]{2,1,0:T(8,128)(2,1)S(1)}, f32[6,1,256]{2,1,0:T(1,128)S(1)}) custom-call(bf16[1024,1536]{1,0:T(8,128)(2,1)} %train.1, bf16[6,256,256]{2,1,0:T(8,128)(2,1)} %precond.1, s32[6]{0:T(128)} %kind.1, f32[7]{0:T(128)} %scale.1), custom_call_target="tpu_custom_call" | custom-call | bytes 6291456 | tf_op jit(solution)/shard_map/stage/pallas_call | solution.py:139
  7.5 0.0 collective-permute-done.2.refs_1_
  7.5 0.0 collective-permute-done.3.refs_2_
  7.5 0.0 copy-done
  7.5 0.8 %early_scores.1.refs_5_ = f32[4,16,1024]{2,1,0:T(8,128)S(1)} custom-call(bf16[16,1536]{1,0:T(8,128)(2,1)S(1)} %copy-done, bf16[16,1536]{1,0:T(8,128)(2,1)S(1)} %collective-permute-done.2.refs_1_, bf16[16,1536]{1,0:T(8,128)(2,1)S(1)} %collective-permute-done.3.refs_2_, bf16[1536,1024]{1,0:T(8,128)(2,1)S(1)} %get-tuple-element.8.refs_3_.refs_2_, ...), custom_call_target="tpu_custom_call" | custom-call | tf_op jit(solution)/shard_map/early_scores/pallas_call | solution.py:166
  8.3 0.0 collective-permute-done.refs_0_
  8.3 0.0 collective-permute-done.1.refs_1_
  8.3 0.8 %late_scores.1 = f32[4,16,1024]{2,1,0:T(8,128)S(1)} custom-call(bf16[16,1536]{1,0:T(8,128)(2,1)S(1)} %collective-permute-done.refs_0_, bf16[16,1536]{1,0:T(8,128)(2,1)S(1)} %collective-permute-done.1.refs_1_, bf16[1536,1024]{1,0:T(8,128)(2,1)S(1)} %get-tuple-element.8.refs_3_.refs_2_, bf16[6,256,256]{2,1,0:T(8,128)(2,1)S(1)} %get-tuple-element.9.refs_4_.refs_3_, ...), custom_call_target="tpu_custom_call" | custom-call | tf_op jit(solution)/shard_map/late_scores/pallas_call | solution.py:174
  9.2 0.7 %collective-permute-start.5 = (f32[16,1024]{1,0:T(8,128)S(1)}, f32[16,1024]{1,0:T(8,128)S(1)}, u32[]{:S(2)}, u32[]{:S(2)}) collective-permute-start(f32[16,1024]{1,0:T(8,128)S(1)} %slice_bitcast_fusion), channel_id=1, source_target_pairs={{0,4},{4,0},{1,5},{5,1},{2,6},{6,2},{3,7},{7,3},{8,12},{12,8},{9,1... | collective-permute-start | bytes 196616 | tf_op jit(solution)/shard_map/ppermute | solution.py:196
  9.9 1.2 %collective-permute-start.4 = (bf16[16,1024]{1,0:T(8,128)(2,1)S(1)}, bf16[16,1024]{1,0:T(8,128)(2,1)S(1)}, u32[]{:S(2)}, u32[]{:S(2)}) collective-permute-start(bf16[16,1024]{1,0:T(8,128)(2,1)S(1)} %fusion.4), channel_id=1, source_target_pairs={{0,16},{8,24},{16,8},{24,0},{1,17},{9,25},{17,9},{25,1},{2,18},{10... | collective-permute-start | bytes 98312 | tf_op jit(solution)/shard_map/ppermute | solution.py:200
  11.0 0.0 collective-permute-done.5
  11.1 1.2 %collective-permute-start.6 = (bf16[16,1024]{1,0:T(8,128)(2,1)S(1)}, bf16[16,1024]{1,0:T(8,128)(2,1)S(1)}, u32[]{:S(2)}, u32[]{:S(2)}) collective-permute-start(bf16[16,1024]{1,0:T(8,128)(2,1)S(1)} %fusion.1), channel_id=1, source_target_pairs={{0,28},{4,8},{8,20},{12,0},{16,4},{20,24},{24,12},{28,16},{1,29},{... | collective-permute-start | bytes 98312 | tf_op jit(solution)/shard_map/ppermute | solution.py:202
  12.3 0.4 %collective-permute-done.4 = bf16[16,1024]{1,0:T(8,128)(2,1)S(1)} collective-permute-done((bf16[16,1024]{1,0:T(8,128)(2,1)S(1)}, bf16[16,1024]{1,0:T(8,128)(2,1)S(1)}, u32[]{:S(2)}, u32[]{:S(2)}) %collective-permute-start.4) | collective-permute-done | bytes 32800 | tf_op jit(solution)/shard_map/ppermute | solution.py:200
  12.6 2.7 %collective-permute-done.6 = bf16[16,1024]{1,0:T(8,128)(2,1)S(1)} collective-permute-done((bf16[16,1024]{1,0:T(8,128)(2,1)S(1)}, bf16[16,1024]{1,0:T(8,128)(2,1)S(1)}, u32[]{:S(2)}, u32[]{:S(2)}) %collective-permute-start.6) | collective-permute-done | bytes 32800 | tf_op jit(solution)/shard_map/ppermute | solution.py:202
  15.4 0.1 collective-permute-start.7
  15.5 1.2 %collective-permute-done.7 = f32[8,1024]{1,0:T(8,128)S(1)} collective-permute-done((f32[8,1024]{1,0:T(8,128)S(1)}, f32[8,1024]{1,0:T(8,128)S(1)}, u32[]{:S(2)}, u32[]{:S(2)}) %collective-permute-start.7) | collective-permute-done | bytes 32800 | tf_op jit(solution)/shard_map/ppermute | solution.py:196
  16.6 0.6 %select_add_fusion = f32[8,1024]{1,0:T(8,128)} fusion(f32[8,1024]{1,0:T(8,128)S(1)} %collective-permute-done.7, f32[16,1024]{1,0:T(8,128)S(1)} %fusion.3, pred[]{:T(512)S(6)} %eq.3), kind=kLoop, calls=%fused_computation.9 | loop fusion | flops 16384 | bytes 131073 | tf_op jit(solution)/shard_map/add | solution.py:206
  (5 shorter events, 0.0 us)
Async XLA Ops:
  0.0 7.5 %copy-start = (bf16[16,1536]{1,0:T(8,128)(2,1)S(1)}, bf16[16,1536]{1,0:T(8,128)(2,1)}, u32[]{:S(2)}) copy-start(bf16[16,1536]{1,0:T(8,128)(2,1)} %refs_0_.1) | copy-start | bytes 147460
  0.0 7.5 %collective-permute-start.2 = (bf16[16,1536]{1,0:T(8,128)(2,1)}, bf16[16,1536]{1,0:T(8,128)(2,1)S(1)}, u32[]{:S(2)}, u32[]{:S(2)}) collective-permute-start(bf16[16,1536]{1,0:T(8,128)(2,1)} %refs_0_.1), channel_id=1, source_target_pairs={{0,1},{1,3},{2,6},{3,0},{4,5},{5,7},{6,2},{7,4},{8,9},{9,11},{10,1... | collective-permute-start | bytes 147464 | tf_op jit(solution)/shard_map/ppermute | solution.py:131
  2.3 5.2 %collective-permute-start.3 = (bf16[16,1536]{1,0:T(8,128)(2,1)}, bf16[16,1536]{1,0:T(8,128)(2,1)S(1)}, u32[]{:S(2)}, u32[]{:S(2)}) collective-permute-start(bf16[16,1536]{1,0:T(8,128)(2,1)} %refs_0_.1), channel_id=1, source_target_pairs={{0,2},{1,5},{2,0},{3,7},{4,6},{5,1},{6,4},{7,3},{8,10},{9,13},{10,... | collective-permute-start | bytes 147464 | tf_op jit(solution)/shard_map/ppermute | solution.py:131
  3.3 5.0 %collective-permute-start = (bf16[16,1536]{1,0:T(8,128)(2,1)}, bf16[16,1536]{1,0:T(8,128)(2,1)S(1)}, u32[]{:S(2)}, u32[]{:S(2)}) collective-permute-start(bf16[16,1536]{1,0:T(8,128)(2,1)} %refs_0_.1), channel_id=1, source_target_pairs={{0,3},{1,0},{2,1},{3,2},{4,7},{5,4},{6,5},{7,6},{8,11},{9,8},{10,9... | collective-permute-start | bytes 147464 | tf_op jit(solution)/shard_map/ppermute | solution.py:131
  3.3 5.0 %collective-permute-start.1 = (bf16[16,1536]{1,0:T(8,128)(2,1)}, bf16[16,1536]{1,0:T(8,128)(2,1)S(1)}, u32[]{:S(2)}, u32[]{:S(2)}) collective-permute-start(bf16[16,1536]{1,0:T(8,128)(2,1)} %refs_0_.1), channel_id=1, source_target_pairs={{0,4},{1,2},{2,3},{3,1},{4,0},{5,6},{6,7},{7,5},{8,12},{9,10},{10,... | collective-permute-start | bytes 147464 | tf_op jit(solution)/shard_map/ppermute | solution.py:131
  9.2 1.9 %collective-permute-start.5 = (f32[16,1024]{1,0:T(8,128)S(1)}, f32[16,1024]{1,0:T(8,128)S(1)}, u32[]{:S(2)}, u32[]{:S(2)}) collective-permute-start(f32[16,1024]{1,0:T(8,128)S(1)} %slice_bitcast_fusion), channel_id=1, source_target_pairs={{0,4},{4,0},{1,5},{5,1},{2,6},{6,2},{3,7},{7,3},{8,12},{12,8},{9,1... | collective-permute-start | bytes 196616 | tf_op jit(solution)/shard_map/ppermute | solution.py:196
  9.9 2.8 %collective-permute-start.4 = (bf16[16,1024]{1,0:T(8,128)(2,1)S(1)}, bf16[16,1024]{1,0:T(8,128)(2,1)S(1)}, u32[]{:S(2)}, u32[]{:S(2)}) collective-permute-start(bf16[16,1024]{1,0:T(8,128)(2,1)S(1)} %fusion.4), channel_id=1, source_target_pairs={{0,16},{8,24},{16,8},{24,0},{1,17},{9,25},{17,9},{25,1},{2,18},{10... | collective-permute-start | bytes 98312 | tf_op jit(solution)/shard_map/ppermute | solution.py:200
  11.1 4.3 %collective-permute-start.6 = (bf16[16,1024]{1,0:T(8,128)(2,1)S(1)}, bf16[16,1024]{1,0:T(8,128)(2,1)S(1)}, u32[]{:S(2)}, u32[]{:S(2)}) collective-permute-start(bf16[16,1024]{1,0:T(8,128)(2,1)S(1)} %fusion.1), channel_id=1, source_target_pairs={{0,28},{4,8},{8,20},{12,0},{16,4},{20,24},{24,12},{28,16},{1,29},{... | collective-permute-start | bytes 98312 | tf_op jit(solution)/shard_map/ppermute | solution.py:202
  15.4 1.3 %collective-permute-start.7 = (f32[8,1024]{1,0:T(8,128)S(1)}, f32[8,1024]{1,0:T(8,128)S(1)}, u32[]{:S(2)}, u32[]{:S(2)}) collective-permute-start(f32[8,1024]{1,0:T(8,128)S(1)} %slice_select_fusion), channel_id=1, source_target_pairs={{0,4},{4,0},{1,5},{5,1},{2,6},{6,2},{3,7},{7,3},{8,12},{12,8},{9,1... | collective-permute-start | bytes 98312 | tf_op jit(solution)/shard_map/ppermute | solution.py:196
